TPU v7x, 512 devices: a whole 4x4x16 slice. The times are simulated.
512 devices in a mesh: dp: 2 (over core), ctx: 64 (over z, y), tp: 4 (over x).
Axes of the slice: x: 4, y: 4, z: 16, core: 2. Of those that a mesh axis runs over, the one named last changes fastest.
Arguments:
- query_proj: bfloat16 [2, 8192, 8192], P('dp', 'tp', 'ctx'), may hold values from -6 to 6
- key_proj: bfloat16 [2, 8192, 8192], P('dp', 'tp', 'ctx'), may hold values from -6 to 6
- value_proj: bfloat16 [2, 8192, 8192], P('dp', 'tp', 'ctx'), may hold values from -6 to 6
- out_grad: bfloat16 [2, 8192, 8192], P('dp', ('ctx', 'tp')), may hold values from -6 to 6
- filter_taps: bfloat16 [4, 2048, 8192], P('tp', 'ctx'), may hold values from -1 to 1
- skip_gain: float32 [4, 2048], P('tp'), may hold values from -3 to 3
Outputs:
- query_grad: bfloat16 [2, 8192, 8192], P('dp', 'tp', 'ctx')
- key_grad: bfloat16 [2, 8192, 8192], P('dp', 'tp', 'ctx')
- value_grad: bfloat16 [2, 8192, 8192], P('dp', 'tp', 'ctx')
- filter_grad: float32 [4, 2048, 8192], P('tp', 'ctx', 'dp')
All inputs are finite; a program needn't handle non-finite values.
Results may differ from a plain program's by a relative error of at most 0.01.
Values may be sent and summed in bfloat16 or wider, within the bound.
No kernel may reach another device: no remote copies, remote signals or barrier semaphores. Data moves between devices by JAX's collectives and lax.ppermute only.
A program may use at most 64 MiB of HBM per device.

v0:
```python
import math

import jax
import jax.numpy as jnp
from jax import lax
from jax.sharding import PartitionSpec as P


def angle_table(row_count, col_count, modulus):
    row_index = lax.broadcasted_iota(jnp.int32, (row_count, col_count), 0)
    col_index = lax.broadcasted_iota(jnp.int32, (row_count, col_count), 1)
    product = row_index * col_index % modulus
    return product.astype(jnp.float32) * (2.0 * math.pi / modulus)


def make_tables(block_rows, local_len):
    half_rows = block_rows // 2
    angle_fwd = angle_table(block_rows, half_rows, block_rows)
    fwd_rows = jnp.concatenate([jnp.cos(angle_fwd), -jnp.sin(angle_fwd)], axis=0).astype(
        jnp.bfloat16
    )
    angle_twid = angle_table(block_rows, local_len, block_rows * local_len)
    twid_cos = jnp.cos(angle_twid)
    twid_sin = -jnp.sin(angle_twid)
    angle_small = angle_table(local_len, local_len, local_len)
    cos_small = jnp.cos(angle_small)
    sin_small = -jnp.sin(angle_small)
    mat_fwd = jnp.concatenate(
        [
            jnp.concatenate([cos_small, sin_small], axis=1),
            jnp.concatenate([-sin_small, cos_small], axis=1),
        ],
        axis=0,
    ).astype(jnp.bfloat16)
    mat_inv = jnp.concatenate(
        [
            jnp.concatenate([cos_small, -sin_small], axis=1),
            jnp.concatenate([sin_small, cos_small], axis=1),
        ],
        axis=0,
    ).astype(jnp.bfloat16)
    angle_back = angle_table(half_rows, block_rows, block_rows)
    back_rows = jnp.concatenate([jnp.cos(angle_back), -jnp.sin(angle_back)], axis=1).astype(
        jnp.bfloat16
    )
    return (fwd_rows, twid_cos, twid_sin, mat_fwd, mat_inv, back_rows)


def finish_forward(section_rows, twid_cos, twid_sin, mat_fwd):
    row_split = section_rows.shape[0] // 2
    real_rows = section_rows[:row_split]
    imag_rows = section_rows[row_split:]
    tcos = twid_cos[:, None, :]
    tsin = twid_sin[:, None, :]
    mixed = jnp.concatenate(
        [real_rows * tcos - imag_rows * tsin, real_rows * tsin + imag_rows * tcos], axis=-1
    ).astype(jnp.bfloat16)
    result = jnp.einsum("kcj,jq->kcq", mixed, mat_fwd, preferred_element_type=jnp.float32)
    col_split = result.shape[-1] // 2
    return (result[..., :col_split], result[..., col_split:])


def inverse_rows(spec_real, spec_imag, tables, factor, form):
    fwd_rows, twid_cos, twid_sin, mat_fwd, mat_inv, back_rows = tables
    joined = jnp.concatenate([spec_real, spec_imag], axis=-1).astype(jnp.bfloat16)
    mixed = jnp.einsum("kcj,jq->kcq", joined, mat_inv, preferred_element_type=jnp.float32)
    col_split = mixed.shape[-1] // 2
    real_part = mixed[..., :col_split]
    imag_part = mixed[..., col_split:]
    tcos = twid_cos[:, None, :]
    tsin = twid_sin[:, None, :]
    stacked = jnp.concatenate(
        [real_part * tcos + imag_part * tsin, imag_part * tcos - real_part * tsin], axis=0
    ).astype(jnp.bfloat16)
    return jnp.einsum(form, back_rows, stacked, preferred_element_type=jnp.float32) * factor


def local(query_proj, key_proj, value_proj, out_grad, filter_taps, skip_gain):
    ctx_count = lax.axis_size("ctx")
    dp_count = lax.axis_size("dp")
    queries = query_proj[0]
    keys_local = key_proj[0]
    values_local = value_proj[0]
    local_len = queries.shape[1]
    block_rows = 2 * ctx_count
    tables = make_tables(block_rows, local_len)
    fwd_rows, twid_cos, twid_sin, mat_fwd, mat_inv, back_rows = tables
    grad_rows = lax.all_to_all(out_grad[0], "tp", split_axis=1, concat_axis=0, tiled=True)
    grad_tokens = jnp.transpose(grad_rows)
    gated_in = (keys_local.astype(jnp.float32) * values_local.astype(jnp.float32)).astype(
        jnp.bfloat16
    )
    gate_grad = (grad_tokens.astype(jnp.float32) * queries.astype(jnp.float32)).astype(jnp.bfloat16)
    gated_cols, grad_cols = (
        lax.all_to_all(gated_in[None], "ctx", split_axis=1, concat_axis=0, tiled=True),
        lax.all_to_all(gate_grad[None], "ctx", split_axis=1, concat_axis=0, tiled=True),
    )
    filter_local = filter_taps[0]
    channel_count = filter_local.shape[0]
    taps_shaped = filter_local.reshape(channel_count, ctx_count, local_len)
    filter_section = jnp.einsum(
        "kn,cnq->kcq", fwd_rows, taps_shaped, preferred_element_type=jnp.float32
    )
    filt_re, filt_im = finish_forward(filter_section, twid_cos, twid_sin, mat_fwd)
    gated_re, gated_im = finish_forward(
        jnp.einsum("kn,ncq->kcq", fwd_rows, gated_cols, preferred_element_type=jnp.float32),
        twid_cos,
        twid_sin,
        mat_fwd,
    )
    grad_re, grad_im = finish_forward(
        jnp.einsum("kn,ncq->kcq", fwd_rows, grad_cols, preferred_element_type=jnp.float32),
        twid_cos,
        twid_sin,
        mat_fwd,
    )
    factor = 1.0 / (block_rows * local_len)
    conv_cols = inverse_rows(
        filt_re * gated_re - filt_im * gated_im,
        filt_re * gated_im + filt_im * gated_re,
        tables,
        factor,
        "mk,kcq->mcq",
    ).astype(jnp.bfloat16)
    corr_cols = inverse_rows(
        filt_re * grad_re + filt_im * grad_im,
        filt_re * grad_im - filt_im * grad_re,
        tables,
        factor,
        "mk,kcq->mcq",
    ).astype(jnp.bfloat16)
    conv_tokens, corr_tokens = (
        lax.all_to_all(conv_cols, "ctx", split_axis=0, concat_axis=1, tiled=True),
        lax.all_to_all(corr_cols, "ctx", split_axis=0, concat_axis=1, tiled=True),
    )
    lag_part = inverse_rows(
        gated_re * grad_re + gated_im * grad_im,
        gated_re * grad_im - gated_im * grad_re,
        tables,
        factor,
        "mk,kcq->cmq",
    )
    lag_total = lax.psum_scatter(
        lag_part.astype(jnp.bfloat16), "dp", scatter_dimension=1, tiled=True
    ).astype(jnp.float32)
    grad_scale = 1.0 / math.sqrt(dp_count * ctx_count * local_len)
    filter_out = (lag_total * grad_scale).reshape(1, channel_count, -1)
    skip_local = skip_gain[0][:, None]
    conv_rows = conv_tokens[0].astype(jnp.float32)
    corr_rows = corr_tokens[0].astype(jnp.float32)
    query_out = (
        grad_tokens.astype(jnp.float32) * (conv_rows + skip_local * gated_in.astype(jnp.float32))
    ).astype(jnp.bfloat16)
    gated_total = corr_rows + skip_local * gate_grad.astype(jnp.float32)
    key_out = (gated_total * values_local.astype(jnp.float32)).astype(jnp.bfloat16)
    value_out = (gated_total * keys_local.astype(jnp.float32)).astype(jnp.bfloat16)
    return (query_out[None], key_out[None], value_out[None], filter_out)


def solution(mesh):
    in_specs = (
        P("dp", "tp", "ctx"),
        P("dp", "tp", "ctx"),
        P("dp", "tp", "ctx"),
        P("dp", ("ctx", "tp"), None),
        P("tp", "ctx", None),
        P("tp", None),
    )
    out_specs = (
        P("dp", "tp", "ctx"),
        P("dp", "tp", "ctx"),
        P("dp", "tp", "ctx"),
        P("tp", "ctx", "dp"),
    )
    return jax.shard_map(local, mesh=mesh, in_specs=in_specs, out_specs=out_specs, check_vma=False)
```

profile of v0, /device:TPU:2, one launch (start us, length us, event | category | flops | bytes accessed | tf_op | source)
XLA Modules:
  0.0 231.8 jit_solution(5248538063270674360)
XLA Ops:
  7.2 1.5 all_to_all.17
  8.7 1.1 copy.82
  9.8 9.3 %all-to-all-start = ((bf16[32,4,2048]{2,0,1:T(8,128)(2,1)}), bf16[32,4,2048]{2,0,1:T(8,128)(2,1)S(1)}, u32[]{:S(2)}, u32[]{:S(2)}) async-start(bf16[32,4,2048]{2,0,1:T(8,128)(2,1)} %copy.82), calls=%async_computation | async-start | bytes 1048576 | tf_op jit(solution)/shard_map/all_to_all | solution.py:88
  19.1 0.2 copy.86
  19.4 0.2 copy.87
  19.6 0.1 fusion.63
  19.7 0.8 copy.88
  20.5 0.5 broadcast.96
  21.0 11.5 %reduce.1 = bf16[2048,128]{1,0:T(8,128)(2,1)S(1)} reduce(bf16[2048,1,128]{2,1,0:T(2,128)(2,1)S(1)} %bitcast.89, bf16[]{:T(256)} %broadcast.96), dimensions={1}, to_apply=%bitcast.81.reduce_sub_computation | reduce | bytes 1048578
  32.5 0.9 reshape.80
  33.5 14.7 %all-to-all-start.1 = ((bf16[64,2,2048]{2,1,0:T(2,128)(2,1)}), bf16[64,2,2048]{2,1,0:T(2,128)(2,1)}, u32[]{:S(2)}, u32[]{:S(2)}) async-start(bf16[64,2,2048]{2,1,0:T(2,128)(2,1)} %reshape.80), calls=%async_computation.1 | async-start | bytes 1048576 | tf_op jit(solution)/shard_map/all_to_all | solution.py:95
  48.1 0.2 copy.96
  48.4 0.1 fusion.64
  48.5 0.8 copy.97
  49.3 12.3 %reduce = bf16[2048,128]{1,0:T(8,128)(2,1)} reduce(bf16[2048,1,128]{2,1,0:T(2,128)(2,1)S(1)} %bitcast.90, bf16[]{:T(256)} %broadcast.96), dimensions={1}, to_apply=%bitcast.83.reduce_sub_computation | reduce | bytes 1048578
  61.6 2.0 reshape.82
  63.6 16.5 %all-to-all-done.1 = bf16[64,2,2048]{2,1,0:T(2,128)(2,1)} async-done(((bf16[64,2,2048]{2,1,0:T(2,128)(2,1)}), bf16[64,2,2048]{2,1,0:T(2,128)(2,1)}, u32[]{:S(2)}, u32[]{:S(2)}) %all-to-all-start.1) | async-done | bytes 524320 | tf_op jit(solution)/shard_map/all_to_all | solution.py:95
  80.1 6.3 %all-to-all-start.3 = ((bf16[64,2,2048]{2,1,0:T(2,128)(2,1)}), bf16[64,2,2048]{2,1,0:T(2,128)(2,1)}, u32[]{:S(2)}, u32[]{:S(2)}) async-start(bf16[64,2,2048]{2,1,0:T(2,128)(2,1)} %reshape.82), calls=%async_computation.3 | async-start | bytes 1048576 | tf_op jit(solution)/shard_map/all_to_all | solution.py:96
  86.4 0.3 sine_negate_fusion
  86.6 0.1 copy.84
  86.7 0.3 fusion.101
  87.0 0.1 copy.83
  87.1 0.1 copy.122
  87.2 0.2 negate_convert_fusion.1
  87.4 0.3 fusion.100
  87.7 0.2 negate_convert_fusion.2
  87.8 0.3 negate_convert_fusion
  88.1 2.7 %fusion.108 = f32[256,32,128]{0,2,1:T(8,128)} fusion(bf16[32,64,128]{2,1,0:T(8,128)(2,1)S(1)} %bitcast.93, bf16[128,64]{0,1:T(8,128)(2,1)S(1)} %get-tuple-element.47, bf16[128,64]{0,1:T(8,128)(2,1)S(1)} %get-tuple-element.48), kind=kOutput, calls=%fused_computation.140 | convolution fusion | flops 134283264 | bytes 4751360 | tf_op jit(solution)/shard_map/kn,cnq->kcq/dot_general | solution.py:101
  90.8 3.6 %reshape.81 = bf16[2048,1,128]{2,1,0:T(2,128)(2,1)S(1)} reshape(bf16[64,2,2048]{2,1,0:T(2,128)(2,1)} %all-to-all-done.1) | data formatting | bytes 1048576
  94.5 2.7 %fusion.70 = f32[256,32,128]{0,2,1:T(8,128)} fusion(bf16[64,32,128]{2,1,0:T(8,128)(2,1)S(1)} %bitcast.92, bf16[128,64]{0,1:T(8,128)(2,1)S(1)} %get-tuple-element.47, bf16[128,64]{0,1:T(8,128)(2,1)S(1)} %get-tuple-element.48), kind=kOutput, calls=%fused_computation.82 | convolution fusion | flops 134283264 | bytes 4751360 | tf_op jit(solution)/shard_map/kn,ncq->kcq/dot_general | solution.py:106
  97.3 20.8 %all-to-all-done.3 = bf16[64,2,2048]{2,1,0:T(2,128)(2,1)} async-done(((bf16[64,2,2048]{2,1,0:T(2,128)(2,1)}), bf16[64,2,2048]{2,1,0:T(2,128)(2,1)}, u32[]{:S(2)}, u32[]{:S(2)}) %all-to-all-start.3) | async-done | bytes 524320 | tf_op jit(solution)/shard_map/all_to_all | solution.py:96
  118.1 3.6 %reshape.83 = bf16[2048,1,128]{2,1,0:T(2,128)(2,1)S(1)} reshape(bf16[64,2,2048]{2,1,0:T(2,128)(2,1)} %all-to-all-done.3) | data formatting | bytes 1048576
  121.8 0.8 fusion.68
  122.5 1.4 copy-done
  124.0 3.5 %subtract_convert_fusion.4 = (bf16[128,32,128]{0,2,1:T(8,128)(2,1)S(1)}, bf16[128,32,128]{0,2,1:T(8,128)(2,1)S(1)}, bf16[128,32,128]{0,2,1:T(8,128)(2,1)S(1)}, b...) fusion(f32[256,32,128]{0,2,1:T(8,128)S(1)} %fusion.68, ...), kind=kLoop, calls=%fused_computation.45 | loop fusion | flops 12582912 | bytes 19005440 | tf_op jit(solution)/shard_map/convert.16
  127.5 0.8 fusion.16
  128.3 0.8 fusion.4
  129.0 0.8 fusion
  129.8 0.7 add_convert_fusion.3
  130.5 1.4 add_convert_fusion.1
  131.9 0.8 fusion.28
  132.7 0.8 fusion.8
  133.4 0.8 fusion.20
  134.2 3.6 %add_convert_fusion = (bf16[128,32,128]{0,2,1:T(8,128)(2,1)}, bf16[128,32,128]{0,2,1:T(8,128)(2,1)}, bf16[128,32,128]{0,2,1:T(8,128)(2,1)}, bf16[128,32,128]{0,2...) fusion(f32[128,32,256]{0,2,1:T(8,128)S(1)} %fusion.28, f32[128,128]{0,1:T(8,128)S(1)} %copy.84, ...), kind=kLoop, calls=%fused_computation.37 | loop fusion | flops 12582912 | bytes 19005440 | tf_op jit(solution)/shard_map/convert.8
  137.8 0.8 fusion.51
  138.5 1.1 copy.103
  139.7 5.8 %all-to-all-start.4 = ((bf16[64,32,128]{2,1,0:T(8,128)(2,1)}), bf16[64,32,128]{2,1,0:T(8,128)(2,1)S(1)}, u32[]{:S(2)}, u32[]{:S(2)}) async-start(bf16[64,32,128]{2,1,0:T(8,128)(2,1)} %copy.103), calls=%async_computation.4 | async-start | bytes 1048576 | tf_op jit(solution)/shard_map/all_to_all | solution.py:134
  145.5 2.3 fusion.48
  147.8 1.1 copy.94
  148.9 28.6 %all-to-all-done.4 = bf16[64,32,128]{2,1,0:T(8,128)(2,1)S(1)} async-done(((bf16[64,32,128]{2,1,0:T(8,128)(2,1)}), bf16[64,32,128]{2,1,0:T(8,128)(2,1)S(1)}, u32[]{:S(2)}, u32[]{:S(2)}) %all-to-all-start.4) | async-done | bytes 524320 | tf_op jit(solution)/shard_map/all_to_all | solution.py:134
  177.6 6.1 %all-to-all-start.2 = ((bf16[64,32,128]{2,1,0:T(8,128)(2,1)}), bf16[64,32,128]{2,1,0:T(8,128)(2,1)}, u32[]{:S(2)}, u32[]{:S(2)}) async-start(bf16[64,32,128]{2,1,0:T(8,128)(2,1)} %copy.94), calls=%async_computation.2 | async-start | bytes 1048576 | tf_op jit(solution)/shard_map/all_to_all | solution.py:133
  183.7 3.1 %fusion.57 = bf16[32,64,128]{2,1,0:T(8,128)(2,1)} fusion(bf16[128,32,128]{0,2,1:T(8,128)(2,1)} %get-tuple-element.23, bf16[128,32,128]{0,2,1:T(8,128)(2,1)} %get-tuple-element.22, bf16[64,128]{1,0:T(8,128)(2,1)S(1)} %get-tuple-element.51, bf16[64,128]{1,0:T(8,128)(2,1)S(1)} %get-tuple-element.52), kind=kOutput, calls=%fused_computation.66 | convolution fusion | flops 139001856 | bytes 2654208 | tf_op jit(solution)/shard_map/mk,kcq->cmq/dot_general | solution.py:75
  186.8 20.2 %reduce-scatter.2.cloned.1.call-done = bf16[32,32,128]{2,1,0:T(8,128)(2,1)} async-done(((bf16[32,64,128]{2,1,0:T(8,128)(2,1)}), bf16[32,32,128]{2,1,0:T(8,128)(2,1)}) %reduce-scatter.2.cloned.1.call-update) | async-done | bytes 262160 | tf_op jit(solution)/shard_map/reduce_scatter | solution.py:143
  207.0 1.0 convert_multiply_fusion.2
  208.0 0.9 reshape.69
  208.9 1.1 bitcast_convert_fusion
  210.0 1.3 copy.104
  211.3 4.2 %all-to-all-done.2 = bf16[64,32,128]{2,1,0:T(8,128)(2,1)} async-done(((bf16[64,32,128]{2,1,0:T(8,128)(2,1)}), bf16[64,32,128]{2,1,0:T(8,128)(2,1)}, u32[]{:S(2)}, u32[]{:S(2)}) %all-to-all-start.2) | async-done | bytes 524320 | tf_op jit(solution)/shard_map/all_to_all | solution.py:133
  215.6 1.1 bitcast_convert_fusion.1
  216.7 1.3 copy.95
  218.0 2.9 %fusion.67 = (bf16[1,2048,128]{1,2,0:T(8,128)(2,1)S(1)}, bf16[1,2048,128]{1,2,0:T(8,128)(2,1)S(1)}, bf16[2048,128]{0,1:T(8,128)(2,1)}) fusion(bf16[1,2048,128]{1,2,0:T(8,128)(2,1)S(1)} %copy.86, f32[2048,128]{0,1:T(8,128)} %copy.104, bf16[2048,128]{0,1:T(8,128)(2,1)S(1)} %fusion.64, f32[2048]{0:T(1024)S(1)} %bitcast.96, bf16[1,2048,128]{1,2,0:T(8,128)(2,1)S(1)} %copy.87, ...), kind=kLoop, calls=%fused_computation.77 | loop fusion | flops 4456448 | bytes 5775360 | tf_op jit(solution)/shard_map/broadcast_in_dim | solution.py:157
  220.9 2.0 copy.108
  222.9 1.0 copy.109
  223.9 1.0 copy.110
  (18 shorter events, 0.2 us)
Async XLA Ops:
  7.2 12.0 %copy-start.2 = (bf16[1,2048,128]{2,1,0:T(8,128)(2,1)S(1)}, bf16[1,2048,128]{2,1,0:T(8,128)(2,1)}, u32[]{:S(2)}) copy-start(bf16[1,2048,128]{2,1,0:T(8,128)(2,1)} %param.7) | copy-start | bytes 1572868
  7.2 12.2 %copy-start.3 = (bf16[1,2048,128]{2,1,0:T(8,128)(2,1)S(1)}, bf16[1,2048,128]{2,1,0:T(8,128)(2,1)}, u32[]{:S(2)}) copy-start(bf16[1,2048,128]{2,1,0:T(8,128)(2,1)} %param.8) | copy-start | bytes 1572868
  9.8 23.7 %all-to-all-start = ((bf16[32,4,2048]{2,0,1:T(8,128)(2,1)}), bf16[32,4,2048]{2,0,1:T(8,128)(2,1)S(1)}, u32[]{:S(2)}, u32[]{:S(2)}) async-start(bf16[32,4,2048]{2,0,1:T(8,128)(2,1)} %copy.82), calls=%async_computation | async-start | bytes 1048576 | tf_op jit(solution)/shard_map/all_to_all | solution.py:88
  32.5 15.6 %copy-start.4 = (bf16[1,2048,128]{2,1,0:T(8,128)(2,1)S(1)}, bf16[1,2048,128]{2,1,0:T(8,128)(2,1)}, u32[]{:S(2)}) copy-start(bf16[1,2048,128]{2,1,0:T(8,128)(2,1)} %param.6) | copy-start | bytes 1572868
  33.5 46.6 %all-to-all-start.1 = ((bf16[64,2,2048]{2,1,0:T(2,128)(2,1)}), bf16[64,2,2048]{2,1,0:T(2,128)(2,1)}, u32[]{:S(2)}, u32[]{:S(2)}) async-start(bf16[64,2,2048]{2,1,0:T(2,128)(2,1)} %reshape.80), calls=%async_computation.1 | async-start | bytes 1048576 | tf_op jit(solution)/shard_map/all_to_all | solution.py:95
  61.6 25.5 %copy-start.5 = (bf16[1,32,8192]{2,1,0:T(8,128)(2,1)S(1)}, bf16[1,32,8192]{2,1,0:T(8,128)(2,1)}, u32[]{:S(2)}) copy-start(bf16[1,32,8192]{2,1,0:T(8,128)(2,1)} %param.10) | copy-start | bytes 1572868
  80.1 38.0 %all-to-all-start.3 = ((bf16[64,2,2048]{2,1,0:T(2,128)(2,1)}), bf16[64,2,2048]{2,1,0:T(2,128)(2,1)}, u32[]{:S(2)}, u32[]{:S(2)}) async-start(bf16[64,2,2048]{2,1,0:T(2,128)(2,1)} %reshape.82), calls=%async_computation.3 | async-start | bytes 1048576 | tf_op jit(solution)/shard_map/all_to_all | solution.py:96
  121.8 2.2 copy-start
  139.7 37.9 %all-to-all-start.4 = ((bf16[64,32,128]{2,1,0:T(8,128)(2,1)}), bf16[64,32,128]{2,1,0:T(8,128)(2,1)S(1)}, u32[]{:S(2)}, u32[]{:S(2)}) async-start(bf16[64,32,128]{2,1,0:T(8,128)(2,1)} %copy.103), calls=%async_computation.4 | async-start | bytes 1048576 | tf_op jit(solution)/shard_map/all_to_all | solution.py:134
  177.6 9.3 %copy-start.1 = (bf16[64,32,128]{2,1,0:T(8,128)(2,1)}, bf16[64,32,128]{2,1,0:T(8,128)(2,1)S(1)}, u32[]{:S(2)}) copy-start(bf16[64,32,128]{2,1,0:T(8,128)(2,1)S(1)} %all-to-all-done.4) | copy-start | bytes 1572868
  177.6 38.0 %all-to-all-start.2 = ((bf16[64,32,128]{2,1,0:T(8,128)(2,1)}), bf16[64,32,128]{2,1,0:T(8,128)(2,1)}, u32[]{:S(2)}, u32[]{:S(2)}) async-start(bf16[64,32,128]{2,1,0:T(8,128)(2,1)} %copy.94), calls=%async_computation.2 | async-start | bytes 1048576 | tf_op jit(solution)/shard_map/all_to_all | solution.py:133
  183.7 23.3 %reduce-scatter.2.cloned.1.call-start = ((), (), s32[]{:S(2)}) async-start(), calls=%async_computation.6 | async-start | bytes 786432 | tf_op jit(solution)/shard_map/reduce_scatter | solution.py:143
  211.3 6.7 %copy-start.6 = (f32[1,2048]{1,0:T(1,128)S(1)}, f32[1,2048]{1,0:T(1,128)}, u32[]{:S(2)}) copy-start(f32[1,2048]{1,0:T(1,128)} %param.11) | copy-start | bytes 24580
Sparse Core Ops, SparseCore 0:
  187.9 19.0 reduce-scatter.1
where the time goes:
time: 233 us; the launch traced here: 232 us
  waiting for transfers between devices  90.3 us (39%)
  starting transfers between devices  42.3 us (18%)
  other arithmetic  40.8 us (18%)
  local copies, waits for them, and re-layouts  27.2 us (12%)
  matrix products  16.9 us (7%)
  between operations  14.3 us (6%)
    all_to_all x1, waiting for transfers between devices, local(): lax.all_to_all(corr_cols, 'ctx', split_axis=0, concat_axis=1, tiled=True)  28.6 us
    unnamed x2, other arithmetic  23.9 us
    all_to_all x1, waiting for transfers between devices, local(): lax.all_to_all(gate_grad[None], 'ctx', split_axis=1, concat_axis=0, tiled...  20.8 us
    reduce_scatter x1, waiting for transfers between devices, local(): lax.psum_scatter(lag_part.astype(jnp.bfloat16), 'dp', scatter_dimension=1...  20.2 us
    unnamed x28, local copies, waits for them, and re-layouts  17.1 us
    all_to_all x1, waiting for transfers between devices, local(): lax.all_to_all(gated_in[None], 'ctx', split_axis=1, concat_axis=0, tiled=...  16.5 us
    all_to_all x1, starting transfers between devices, local(): lax.all_to_all(gated_in[None], 'ctx', split_axis=1, concat_axis=0, tiled=...  14.7 us
    another operation x8, other arithmetic  10.1 us
  transfers between devices with their start and end apart: 6, of which 5 were waited for; matrix products, arithmetic and copies ran while one was open for 22% of the time, Pallas kernels for 0%

commit v1 on v0

v1 whole, which is shorter than its diff:
```python
import functools
import math

import jax
import jax.numpy as jnp
import numpy as np
from jax import lax
from jax.experimental import pallas as pl
from jax.experimental.pallas import tpu as pltpu
from jax.sharding import PartitionSpec as P

BF = jnp.bfloat16
F32 = jnp.float32


def angle(rows, cols, modulus):
    product = np.arange(rows)[:, None] * np.arange(cols)[None, :] % modulus
    return product.astype(np.float32) * np.float32(2.0 * math.pi / modulus)


def make_tables(block_rows, local_len, factor):
    half = block_rows // 2
    kept = half + 1
    rows = -(-kept // 16) * 16
    real = (np.arange(rows) < kept).astype(np.float32)[:, None]
    weight = np.where((np.arange(rows) == 0) | (np.arange(rows) == half), 1.0, 2.0)[:, None] * real
    fwd = angle(rows, half, block_rows)
    fwd_rows = np.concatenate([np.cos(fwd) * real, -np.sin(fwd) * real], axis=0)
    back_rows = np.concatenate([np.cos(fwd) * weight, -np.sin(fwd) * weight], axis=0).T * factor
    twid = angle(rows, local_len, block_rows * local_len)
    small = angle(local_len, local_len, local_len)
    c, s = np.cos(small), -np.sin(small)
    mat_fwd = np.block([[c, s], [-s, c]])
    mat_inv = np.block([[c, -s], [s, c]])
    pair = lambda a: np.concatenate([a, a], axis=1)
    return (
        jnp.asarray(fwd_rows, BF),
        jnp.asarray(back_rows, BF),
        jnp.asarray(pair(np.cos(twid)), F32),
        jnp.asarray(pair(-np.sin(twid)), F32),
        jnp.asarray(mat_fwd, BF),
        jnp.asarray(mat_inv, BF),
    )


def dot(a, b):
    return jnp.dot(a, b, preferred_element_type=F32)


def forward(blocks, fwd, tcos, tsin, mat, mixed):
    rows = fwd.shape[0] // 2
    n = blocks[0].shape[-1]
    tc, ts = tcos[...], tsin[...]
    for c in range(0, len(blocks), 2):
        a = dot(fwd[...], jnp.concatenate(blocks[c : c + 2], axis=-1))
        ar, ai = a[:rows], a[rows:]
        re = (ar * tc - ai * ts).astype(BF)
        im = (ar * ts + ai * tc).astype(BF)
        for j in range(2):
            at = pl.ds((c + j) * rows, rows)
            mixed[at, :n] = re[:, j * n : (j + 1) * n]
            mixed[at, n:] = im[:, j * n : (j + 1) * n]
    return dot(mixed[...], mat[...])


def inverse(re, im, back, tcos, tsin, mat):
    rows = back.shape[1] // 2
    n = re.shape[-1]
    tc, ts = tcos[...], tsin[...]
    e = dot(jnp.concatenate([re, im], axis=-1).astype(BF), mat[...])
    out = []
    for c in range(0, e.shape[0], 2 * rows):
        e0, e1 = e[c : c + rows], e[c + rows : c + 2 * rows]
        er = jnp.concatenate([e0[:, :n], e1[:, :n]], axis=-1)
        ei = jnp.concatenate([e0[:, n:], e1[:, n:]], axis=-1)
        g = jnp.concatenate([er * tc + ei * ts, ei * tc - er * ts], axis=0).astype(BF)
        o = dot(back[...], g)
        out += [o[:, :n], o[:, n:]]
    return out


def split(spec):
    n = spec.shape[-1] // 2
    return spec[:, :n], spec[:, n:]


def by_channel(ref):
    a = jnp.swapaxes(ref[...].astype(F32), 0, 1).astype(BF)
    return [a[c] for c in range(a.shape[0])]


def by_block(parts):
    return jnp.swapaxes(jnp.stack(parts), 0, 1).astype(BF)


def conv_kernel(x, taps, fwd, back, tc, ts, mf, mi, conv, f_spec, x_spec, mixed):
    f = forward([taps[c] for c in range(taps.shape[0])], fwd, tc, ts, mf, mixed)
    f_spec[...] = f
    s = forward(by_channel(x), fwd, tc, ts, mf, mixed)
    x_spec[...] = s
    fr, fi = split(f)
    xr, xi = split(s)
    conv[...] = by_block(inverse(fr * xr - fi * xi, fr * xi + fi * xr, back, tc, ts, mi))


def corr_kernel(x, conv, f_spec, fwd, back, tc, ts, mf, mi, both, g_spec, mixed):
    s = forward(by_channel(x), fwd, tc, ts, mf, mixed)
    g_spec[...] = s
    fr, fi = split(f_spec[...])
    gr, gi = split(s)
    both[:, 0] = conv[...]
    both[:, 1] = by_block(inverse(fr * gr + fi * gi, fr * gi - fi * gr, back, tc, ts, mi))


def lag_kernel(x_spec, g_spec, own_rows, away_rows, tc, ts, mi, own, away):
    xr, xi = split(x_spec[...])
    gr, gi = split(g_spec[...])
    rows = own_rows.shape[0]
    both = jnp.concatenate([own_rows[...], away_rows[...]], axis=0)
    parts = inverse(xr * gr + xi * gi, xr * gi - xi * gr, both, tc, ts, mi)
    for c, part in enumerate(parts):
        own[c] = part[:rows]
        away[c] = part[rows:].astype(BF)


def call(body, grid, ins, tables, outs, mixed=None):
    def cut(a, dim):
        block = tuple(s // grid if i == dim else s for i, s in enumerate(a.shape))
        return pl.BlockSpec(block, lambda g: tuple(g if i == dim else 0 for i in range(len(block))))

    def whole(a):
        return pl.BlockSpec(a.shape, lambda g: (0,) * len(a.shape))

    return pl.pallas_call(
        body,
        grid=(grid,),
        in_specs=[cut(a, d) for a, d in ins] + [whole(a) for a in tables],
        out_specs=[cut(a, d) for a, d in outs],
        out_shape=[a for a, _ in outs],
        scratch_shapes=[] if mixed is None else [pltpu.VMEM(mixed, BF)],
        compiler_params=pltpu.CompilerParams(vmem_limit_bytes=40 * 2**20),
        cost_estimate=pl.CostEstimate(flops=2**20, bytes_accessed=2**20, transcendentals=0),
    )(*[a for a, _ in ins], *tables)


def local(query_proj, key_proj, value_proj, out_grad, filter_taps, skip_gain):
    ctx = lax.axis_size("ctx")
    tp = lax.axis_size("tp")
    dp = lax.axis_size("dp")
    q, k, v = query_proj[0], key_proj[0], value_proj[0]
    chans, block = q.shape
    own = chans // ctx
    factor = 1.0 / (2 * ctx * block)
    fwd, back, tc, ts, mf, mi = make_tables(2 * ctx, block, factor)
    x = lax.axis_index("tp")
    core = lax.axis_index("dp")
    grid = 2
    spec = jax.ShapeDtypeStruct((own * tc.shape[0], 2 * block), F32)
    mixed = (spec.shape[0] // grid, 2 * block)

    def exchange(a):
        return lax.all_to_all(a, "ctx", split_axis=0, concat_axis=0, tiled=True)

    gated_in = (k.astype(F32) * v.astype(F32)).astype(BF)
    gated_c = exchange(gated_in.reshape(ctx, own, block))

    rows = out_grad[0]
    rows_per = rows.shape[0]
    parts = []
    for d in range(tp):
        piece = lax.dynamic_slice_in_dim(rows, lax.rem(x + d, tp) * chans, chans, axis=1)
        if d:
            piece = lax.ppermute(piece, "tp", [(j, (j + d) % tp) for j in range(tp)])
        parts.append(piece)
    order = [parts[(tp - 1 - i) % tp] for i in range(2 * tp - 1)]
    ring = jnp.concatenate(order, axis=0)
    grad_rows = lax.dynamic_slice_in_dim(ring, (tp - 1 - x) * rows_per, tp * rows_per, axis=0)
    grad_tokens = jnp.transpose(grad_rows)
    gate_grad = (grad_tokens.astype(F32) * q.astype(F32)).astype(BF)
    gated_c, gate_grad_c = lax.optimization_barrier((gated_c, gate_grad))
    grad_c = exchange(gate_grad_c.reshape(ctx, own, block))

    taps = filter_taps[0].reshape(own, ctx, block)
    tables = (fwd, back, tc, ts, mf, mi)
    block_out = jax.ShapeDtypeStruct((ctx, own, block), BF)
    conv, f_spec, x_spec = call(
        conv_kernel, grid, [(gated_c, 1), (taps, 0)], tables,
        [(block_out, 1), (spec, 0), (spec, 0)], mixed,
    )
    both, g_spec = call(
        corr_kernel, grid, [(grad_c, 1), (conv, 1), (f_spec, 0)], tables,
        [(jax.ShapeDtypeStruct((ctx, 2, own, block), BF), 2), (spec, 0)], mixed,
    )
    both = exchange(both.reshape(ctx, 2 * own, block)).reshape(ctx, 2, own, block)

    halves = back.reshape(dp, ctx // dp, -1)
    half_out = (own, ctx // dp, block)
    lag_own, lag_away = call(
        lag_kernel, grid, [(x_spec, 0), (g_spec, 0)],
        (
            lax.dynamic_index_in_dim(halves, core, keepdims=False),
            lax.dynamic_index_in_dim(halves, lax.rem(core + 1, dp), keepdims=False),
            tc, ts, mi,
        ),
        [(jax.ShapeDtypeStruct(half_out, F32), 0), (jax.ShapeDtypeStruct(half_out, BF), 0)],
    )
    other = lax.ppermute(lag_away, "dp", [(j, (j + 1) % dp) for j in range(dp)])
    grad_scale = 1.0 / math.sqrt(dp * ctx * block)
    filter_out = ((lag_own + other.astype(F32)) * grad_scale).reshape(1, own, -1)

    skip = skip_gain[0][:, None]
    conv_rows = both[:, 0].reshape(chans, block).astype(F32)
    corr_rows = both[:, 1].reshape(chans, block).astype(F32)
    query_out = (grad_tokens.astype(F32) * (conv_rows + skip * gated_in.astype(F32))).astype(BF)
    total = corr_rows + skip * gate_grad.astype(F32)
    key_out = (total * v.astype(F32)).astype(BF)
    value_out = (total * k.astype(F32)).astype(BF)
    return (query_out[None], key_out[None], value_out[None], filter_out)


def solution(mesh):
    assert mesh.shape["dp"] == 2
    in_specs = (
        P("dp", "tp", "ctx"),
        P("dp", "tp", "ctx"),
        P("dp", "tp", "ctx"),
        P("dp", ("ctx", "tp"), None),
        P("tp", "ctx", None),
        P("tp", None),
    )
    out_specs = (
        P("dp", "tp", "ctx"),
        P("dp", "tp", "ctx"),
        P("dp", "tp", "ctx"),
        P("tp", "ctx", "dp"),
    )
    return jax.shard_map(local, mesh=mesh, in_specs=in_specs, out_specs=out_specs, check_vma=False)
```

time: 233 us -> 185 us (0.79)
  the two profiles are of different devices: /device:TPU:2 before, /device:TPU:8 now
where the time goes in v1:
time: 185 us; the launch traced here: 184 us
  waiting for transfers between devices  94.9 us (51%)
  starting transfers between devices  52.3 us (28%)
  local copies, waits for them, and re-layouts  21.1 us (11%)
  other arithmetic  7.7 us (4%)
  Pallas kernels  7.35 us (4%)
    all_to_all x3, waiting for transfers between devices, exchange(): return lax.all_to_all(a, 'ctx', split_axis=0, concat_axis=0, tiled=True)  73.5 us
    all_to_all x3, starting transfers between devices, exchange(): return lax.all_to_all(a, 'ctx', split_axis=0, concat_axis=0, tiled=True)  40.1 us
    ppermute x3, waiting for transfers between devices, local(): piece = lax.ppermute(piece, 'tp', [(j, (j + d) % tp) for j in range(tp)])  19.9 us
    unnamed x45, local copies, waits for them, and re-layouts  11.3 us
    ppermute x3, starting transfers between devices, local(): piece = lax.ppermute(piece, 'tp', [(j, (j + d) % tp) for j in range(tp)])  10.2 us
    pallas_call x3, Pallas kernels, call(): pl.pallas_call(body, grid=(grid,), in_specs=[cut(a, d) for a, d in ins] +...  7.35 us
    concatenate x1, local copies, waits for them, and re-layouts, local(): ring = jnp.concatenate(order, axis=0)  5 us
  transfers between devices with their start and end apart: 7, of which 5 were waited for; matrix products, arithmetic and copies ran while one was open for 6% of the time, Pallas kernels for 2%

profile of v1, /device:TPU:8, one launch (start us, length us, event | category | flops | bytes accessed | tf_op | source)
XLA Modules:
  0.0 184.4 jit_solution(1985630796985890337)
XLA Ops:
  0.6 0.0 copy-start.18
  0.6 2.2 %fusion.6 = bf16[1,2048,128]{2,1,0:T(8,128)(2,1)} fusion(bf16[1,2048,128]{2,1,0:T(8,128)(2,1)} %param.14, bf16[1,2048,128]{2,1,0:T(8,128)(2,1)} %param.13), kind=kLoop, calls=%fused_computation.9 | loop fusion | flops 1048576 | bytes 1572864 | tf_op jit(solution)/shard_map/convert_element_type | solution.py:164
  2.8 18.7 %all-to-all-start = ((bf16[64,32,128]{2,1,0:T(8,128)(2,1)}), bf16[64,32,128]{2,1,0:T(8,128)(2,1)S(1)}, u32[]{:S(2)}, u32[]{:S(2)}) async-start(bf16[64,32,128]{2,1,0:T(8,128)(2,1)} %bitcast.5), calls=%async_computation | async-start | bytes 1048576 | tf_op jit(solution)/shard_map/all_to_all | solution.py:162
  21.6 0.0 copy-done.18
  21.6 0.1 constant_dynamic-slice_fusion
  21.7 0.3 copy.16
  21.9 4.7 %collective-permute-start = (bf16[32,2048]{0,1:T(8,128)(2,1)S(1)}, bf16[32,2048]{0,1:T(8,128)(2,1)S(1)}, u32[]{:S(2)}, u32[]{:S(2)}) collective-permute-start(bf16[32,2048]{0,1:T(8,128)(2,1)S(1)} %bitcast.72), channel_id=1, source_target_pairs={{0,3},{1,0},{2,1},{3,2},{4,7},{5,4},{6,5},{7,6},{8,11},{9,8},{10,9... | collective-permute-start | bytes 393224 | tf_op jit(solution)/shard_map/ppermute | solution.py:173
  26.6 0.3 copy.17
  26.9 2.7 %collective-permute-start.1 = (bf16[32,2048]{0,1:T(8,128)(2,1)S(1)}, bf16[32,2048]{0,1:T(8,128)(2,1)S(1)}, u32[]{:S(2)}, u32[]{:S(2)}) collective-permute-start(bf16[32,2048]{0,1:T(8,128)(2,1)S(1)} %bitcast.73), channel_id=1, source_target_pairs={{0,2},{1,3},{2,0},{3,1},{4,6},{5,7},{6,4},{7,5},{8,10},{9,11},{10,... | collective-permute-start | bytes 393224 | tf_op jit(solution)/shard_map/ppermute | solution.py:173
  29.6 1.0 copy.18
  30.6 2.8 %collective-permute-start.2 = (bf16[32,2048]{0,1:T(8,128)(2,1)}, bf16[32,2048]{0,1:T(8,128)(2,1)S(1)}, u32[]{:S(2)}, u32[]{:S(2)}) collective-permute-start(bf16[32,2048]{0,1:T(8,128)(2,1)} %bitcast.74), channel_id=1, source_target_pairs={{0,1},{1,2},{2,3},{3,0},{4,5},{5,6},{6,7},{7,4},{8,9},{9,10},{10,1... | collective-permute-start | bytes 393224 | tf_op jit(solution)/shard_map/ppermute | solution.py:173
  33.4 1.0 copy.19
  34.4 14.1 %collective-permute-done = bf16[32,2048]{0,1:T(8,128)(2,1)S(1)} collective-permute-done((bf16[32,2048]{0,1:T(8,128)(2,1)S(1)}, bf16[32,2048]{0,1:T(8,128)(2,1)S(1)}, u32[]{:S(2)}, u32[]{:S(2)}) %collective-permute-start) | collective-permute-done | bytes 131104 | tf_op jit(solution)/shard_map/ppermute | solution.py:173
  48.5 0.0 collective-permute-done.1
  48.5 5.9 %collective-permute-done.2 = bf16[32,2048]{0,1:T(8,128)(2,1)S(1)} collective-permute-done((bf16[32,2048]{0,1:T(8,128)(2,1)}, bf16[32,2048]{0,1:T(8,128)(2,1)S(1)}, u32[]{:S(2)}, u32[]{:S(2)}) %collective-permute-start.2) | collective-permute-done | bytes 131104 | tf_op jit(solution)/shard_map/ppermute | solution.py:173
  54.4 5.0 %concatenate.3 = bf16[224,2048]{0,1:T(8,128)(2,1)S(1)} concatenate(bf16[32,2048]{0,1:T(8,128)(2,1)S(1)} %collective-permute-done, bf16[32,2048]{0,1:T(8,128)(2,1)S(1)} %collective-permute-done.1, bf16[32,2048]{0,1:T(8,128)(2,1)S(1)} %collective-permute-done.2, bf16[32,2048]{0,1:T(8,128)(2,1)} %bitcast.71, bf16[32,2048]{0,1:T(8,128)(2,1)S(1)} %collective-permute-done, ...), dimensions={0} | concatenate | bytes 1835008 | tf_op jit(solution)/shard_map/concatenate | solution.py:176
  59.4 0.0 copy-start.14
  59.4 0.0 copy-start.19
  59.4 0.0 copy-start.4
  59.4 0.0 copy-start.6
  59.4 0.0 copy-start.7
  59.4 0.0 copy-start.12
  59.4 0.0 copy-start.13
  59.4 2.5 %fusion.9 = bf16[2048,128]{1,0:T(8,128)(2,1)} fusion(bf16[1,2048,128]{2,1,0:T(8,128)(2,1)} %param.12, bf16[224,2048]{0,1:T(8,128)(2,1)S(1)} %concatenate.3, s32[]{:T(128)S(6)} %select_n.26), kind=kLoop, calls=%fused_computation.15 | loop fusion | flops 1048576 | bytes 1572868 | tf_op jit(solution)/shard_map/convert_element_type | solution.py:179
  62.0 0.0 all-to-all-done.x
  62.0 15.3 %all-to-all-start.1 = ((bf16[64,32,128]{2,1,0:T(8,128)(2,1)}), bf16[64,32,128]{2,1,0:T(8,128)(2,1)}, u32[]{:S(2)}, u32[]{:S(2)}) async-start(bf16[64,32,128]{2,1,0:T(8,128)(2,1)} %bitcast.7), calls=%async_computation.1 | async-start | bytes 1048576 | tf_op jit(solution)/shard_map/all_to_all | solution.py:162
  77.3 0.0 copy-done.19
  77.3 0.1 copy.24
  77.4 0.0 copy-done.14
  77.4 0.0 copy-done.4
  77.4 0.0 copy-done.6
  77.4 0.0 copy-done.7
  77.4 0.0 copy-done.12
  77.4 0.0 copy-done.13
  77.4 0.0 copy-start.8
  77.5 0.9 copy-done.8
  78.4 2.9 %shard_map.147 = (bf16[64,32,128]{2,1,0:T(8,128)(2,1)S(1)}, f32[2560,256]{1,0:T(8,128)S(1)}, f32[2560,256]{1,0:T(8,128)S(1)}) custom-call(bf16[64,32,128]{2,1,0:T(8,128)(2,1)S(1)} %all-to-all-done.x, bf16[32,64,128]{2,1,0:T(8,128)(2,1)S(1)} %bitcast.69, bf16[160,64]{1,0:T(8,128)(2,1)S(1)} %copy-done.12, bf16[64,160]{1,0:T(8,128)(2,1)S(1)} %copy-done.13, ...), custom_call_target="tpu_custom_call" | custom-call | flops 1048576 | bytes 1048576 | tf_op jit(solution)/shard_map/pallas_call | solution.py:134
  81.3 0.0 copy-start.2
  81.3 1.5 copy-done.2
  82.8 0.8 copy-done.10
  83.6 26.5 %all-to-all-done.1.x = bf16[64,32,128]{2,1,0:T(8,128)(2,1)} async-done(((bf16[64,32,128]{2,1,0:T(8,128)(2,1)}), bf16[64,32,128]{2,1,0:T(8,128)(2,1)}, u32[]{:S(2)}, u32[]{:S(2)}) %all-to-all-start.1) | async-done | bytes 524320 | tf_op jit(solution)/shard_map/all_to_all | solution.py:162
  110.1 1.7 copy-done.3
  111.8 0.9 copy-done.9
  112.7 1.0 copy-done.11
  113.7 3.2 %shard_map.148 = (bf16[64,2,32,128]{3,2,1,0:T(8,128)(2,1)S(1)}, f32[2560,256]{1,0:T(8,128)S(1)}) custom-call(bf16[64,32,128]{2,1,0:T(8,128)(2,1)} %all-to-all-done.1.x, bf16[64,32,128]{2,1,0:T(8,128)(2,1)S(1)} %copy-done.11, f32[2560,256]{1,0:T(8,128)S(1)} %copy-done.3, bf16[160,64]{1,0:T(8,128)(2,1)S(1)} %copy-done.12, bf16[64,160]{1,0:T(8,128)(2,1)S(1)} %copy-done.13, ...), custom_call_target="tpu_custom_call" | custom-call | flops 1048576 | bytes 1048576 | tf_op jit(solution)/shard_map/pallas_call | solution.py:134
  116.9 0.0 copy-start
  116.9 1.5 copy-done
  118.4 1.0 copy-done.5
  119.4 6.1 %all-to-all-start.2 = ((bf16[64,64,128]{2,1,0:T(8,128)(2,1)}), bf16[64,64,128]{2,1,0:T(8,128)(2,1)}, u32[]{:S(2)}, u32[]{:S(2)}) async-start(bf16[64,64,128]{2,1,0:T(8,128)(2,1)} %bitcast.70), calls=%async_computation.2 | async-start | bytes 2097152 | tf_op jit(solution)/shard_map/all_to_all | solution.py:162
  125.6 0.0 copy-done.20
  125.6 0.0 copy-start.1
  125.6 1.7 copy-done.1
  127.3 1.2 shard_map.149
  128.6 0.0 copy-start.15
  128.6 0.0 copy-start.16
  128.6 0.0 copy-start.17
  128.6 0.0 copy-start.21
  128.6 2.1 %collective-permute-start.3 = (bf16[32,32,128]{2,1,0:T(8,128)(2,1)S(1)}, bf16[32,32,128]{2,1,0:T(8,128)(2,1)S(1)}, u32[]{:S(2)}, u32[]{:S(2)}) collective-permute-start(bf16[32,32,128]{2,1,0:T(8,128)(2,1)S(1)} %get-tuple-element.21), channel_id=1, source_target_pairs={{0,256},{256,0},{1,257},{257,1},{2,258},{258,2},{3,259},{259,3},{4... | collective-permute-start | bytes 786440 | tf_op jit(solution)/shard_map/ppermute | solution.py:207
  130.7 1.5 collective-permute-done.3
  132.2 0.1 add_multiply_fusion
  132.3 0.9 reshape.49
  133.2 47.0 %all-to-all-done.2 = bf16[64,64,128]{2,1,0:T(8,128)(2,1)} async-done(((bf16[64,64,128]{2,1,0:T(8,128)(2,1)}), bf16[64,64,128]{2,1,0:T(8,128)(2,1)}, u32[]{:S(2)}, u32[]{:S(2)}) %all-to-all-start.2) | async-done | bytes 1048608 | tf_op jit(solution)/shard_map/all_to_all | solution.py:162
  180.2 1.3 fusion.13
  181.5 2.9 %fusion.12 = (bf16[1,2048,128]{2,1,0:T(8,128)(2,1)}, bf16[1,2048,128]{2,1,0:T(8,128)(2,1)}, bf16[1,2048,128]{2,1,0:T(8,128)(2,1)}) fusion(bf16[1,2048,128]{2,1,0:T(8,128)(2,1)S(1)} %copy-done.16, bf16[2048,128]{1,0:T(8,128)(2,1)} %fusion.9, bf16[64,1,32,128]{3,2,1,0:T(8,128)(2,1)S(1)} %get-tuple-element.25, f32[2048]{0:T(1024)S(1)} %bitcast.76, ...), kind=kLoop, calls=%fused_computation.18 | loop fusion | flops 4980736 | bytes 4726788 | tf_op jit(solution)/shard_map/broadcast_in_dim | solution.py:218
  (11 shorter events, 0.0 us)
Async XLA Ops:
  0.6 21.0 %copy-start.18 = (bf16[1,32,8192]{2,1,0:T(8,128)(2,1)S(1)}, bf16[1,32,8192]{2,1,0:T(8,128)(2,1)}, u32[]{:S(2)}) copy-start(bf16[1,32,8192]{2,1,0:T(8,128)(2,1)} %param.15) | copy-start | bytes 1572868
  2.8 59.1 %all-to-all-start = ((bf16[64,32,128]{2,1,0:T(8,128)(2,1)}), bf16[64,32,128]{2,1,0:T(8,128)(2,1)S(1)}, u32[]{:S(2)}, u32[]{:S(2)}) async-start(bf16[64,32,128]{2,1,0:T(8,128)(2,1)} %bitcast.5), calls=%async_computation | async-start | bytes 1048576 | tf_op jit(solution)/shard_map/all_to_all | solution.py:162
  21.9 26.5 %collective-permute-start = (bf16[32,2048]{0,1:T(8,128)(2,1)S(1)}, bf16[32,2048]{0,1:T(8,128)(2,1)S(1)}, u32[]{:S(2)}, u32[]{:S(2)}) collective-permute-start(bf16[32,2048]{0,1:T(8,128)(2,1)S(1)} %bitcast.72), channel_id=1, source_target_pairs={{0,3},{1,0},{2,1},{3,2},{4,7},{5,4},{6,5},{7,6},{8,11},{9,8},{10,9... | collective-permute-start | bytes 393224 | tf_op jit(solution)/shard_map/ppermute | solution.py:173
  26.9 21.6 %collective-permute-start.1 = (bf16[32,2048]{0,1:T(8,128)(2,1)S(1)}, bf16[32,2048]{0,1:T(8,128)(2,1)S(1)}, u32[]{:S(2)}, u32[]{:S(2)}) collective-permute-start(bf16[32,2048]{0,1:T(8,128)(2,1)S(1)} %bitcast.73), channel_id=1, source_target_pairs={{0,2},{1,3},{2,0},{3,1},{4,6},{5,7},{6,4},{7,5},{8,10},{9,11},{10,... | collective-permute-start | bytes 393224 | tf_op jit(solution)/shard_map/ppermute | solution.py:173
  30.6 23.7 %collective-permute-start.2 = (bf16[32,2048]{0,1:T(8,128)(2,1)}, bf16[32,2048]{0,1:T(8,128)(2,1)S(1)}, u32[]{:S(2)}, u32[]{:S(2)}) collective-permute-start(bf16[32,2048]{0,1:T(8,128)(2,1)} %bitcast.74), channel_id=1, source_target_pairs={{0,1},{1,2},{2,3},{3,0},{4,5},{5,6},{6,7},{7,4},{8,9},{9,10},{10,1... | collective-permute-start | bytes 393224 | tf_op jit(solution)/shard_map/ppermute | solution.py:173
  59.4 18.0 %copy-start.14 = (bf16[224,2048]{0,1:T(8,128)(2,1)}, bf16[224,2048]{0,1:T(8,128)(2,1)S(1)}, u32[]{:S(2)}) copy-start(bf16[224,2048]{0,1:T(8,128)(2,1)S(1)} %concatenate.3) | copy-start | bytes 2752516
  59.4 17.9 %copy-start.19 = (bf16[1,32,8192]{2,1,0:T(8,128)(2,1)S(1)}, bf16[1,32,8192]{2,1,0:T(8,128)(2,1)}, u32[]{:S(2)}) copy-start(bf16[1,32,8192]{2,1,0:T(8,128)(2,1)} %param.16) | copy-start | bytes 1572868
  59.4 18.0 %copy-start.4 = (bf16[256,256]{1,0:T(8,128)(2,1)S(1)}, bf16[256,256]{1,0:T(8,128)(2,1)}, u32[]{:S(2)}) copy-start(bf16[256,256]{1,0:T(8,128)(2,1)} %constant.66.clone.mi) | copy-start | bytes 393220
  59.4 18.0 %copy-start.6 = (f32[80,256]{1,0:T(8,128)S(1)}, f32[80,256]{1,0:T(8,128)}, u32[]{:S(2)}) copy-start(f32[80,256]{1,0:T(8,128)} %constant.63.clone.tc) | copy-start | bytes 245764
  59.4 18.0 %copy-start.7 = (f32[80,256]{1,0:T(8,128)S(1)}, f32[80,256]{1,0:T(8,128)}, u32[]{:S(2)}) copy-start(f32[80,256]{1,0:T(8,128)} %constant.64.clone.ts) | copy-start | bytes 245764
  59.4 18.0 %copy-start.12 = (bf16[160,64]{1,0:T(8,128)(2,1)S(1)}, bf16[160,64]{1,0:T(8,128)(2,1)}, u32[]{:S(2)}) copy-start(bf16[160,64]{1,0:T(8,128)(2,1)} %constant.61.clone.fwd) | copy-start | bytes 61444
  59.4 18.0 %copy-start.13 = (bf16[64,160]{1,0:T(8,128)(2,1)S(1)}, bf16[64,160]{1,0:T(8,128)(2,1)}, u32[]{:S(2)}) copy-start(bf16[64,160]{1,0:T(8,128)(2,1)} %constant.62.clone.back) | copy-start | bytes 61444
  62.0 48.1 %all-to-all-start.1 = ((bf16[64,32,128]{2,1,0:T(8,128)(2,1)}), bf16[64,32,128]{2,1,0:T(8,128)(2,1)}, u32[]{:S(2)}, u32[]{:S(2)}) async-start(bf16[64,32,128]{2,1,0:T(8,128)(2,1)} %bitcast.7), calls=%async_computation.1 | async-start | bytes 1048576 | tf_op jit(solution)/shard_map/all_to_all | solution.py:162
  77.4 0.9 copy-start.8
  81.3 1.5 copy-start.2
  82.8 0.8 copy-start.10
  110.1 1.7 copy-start.3
  111.8 0.9 copy-start.9
  112.7 1.0 copy-start.11
  113.7 11.8 %copy-start.20 = (bf16[2,32,160]{2,1,0:T(8,128)(2,1)S(1)}, bf16[2,32,160]{2,1,0:T(8,128)(2,1)}, u32[]{:S(2)}) copy-start(bf16[2,32,160]{2,1,0:T(8,128)(2,1)} %constant.73) | copy-start | bytes 61444
  116.9 1.5 copy-start
  118.4 1.0 copy-start.5
  119.4 60.7 %all-to-all-start.2 = ((bf16[64,64,128]{2,1,0:T(8,128)(2,1)}), bf16[64,64,128]{2,1,0:T(8,128)(2,1)}, u32[]{:S(2)}, u32[]{:S(2)}) async-start(bf16[64,64,128]{2,1,0:T(8,128)(2,1)} %bitcast.70), calls=%async_computation.2 | async-start | bytes 2097152 | tf_op jit(solution)/shard_map/all_to_all | solution.py:162
  125.6 1.7 copy-start.1
  128.6 52.9 %copy-start.15 = (bf16[224,2048]{0,1:T(8,128)(2,1)S(1)}, bf16[224,2048]{0,1:T(8,128)(2,1)}, u32[]{:S(2)}) copy-start(bf16[224,2048]{0,1:T(8,128)(2,1)} %copy-done.14) | copy-start | bytes 2752516
  128.6 52.9 %copy-start.16 = (bf16[1,2048,128]{2,1,0:T(8,128)(2,1)S(1)}, bf16[1,2048,128]{2,1,0:T(8,128)(2,1)}, u32[]{:S(2)}) copy-start(bf16[1,2048,128]{2,1,0:T(8,128)(2,1)} %param.13) | copy-start | bytes 1572868
  128.6 52.9 %copy-start.17 = (bf16[1,2048,128]{2,1,0:T(8,128)(2,1)S(1)}, bf16[1,2048,128]{2,1,0:T(8,128)(2,1)}, u32[]{:S(2)}) copy-start(bf16[1,2048,128]{2,1,0:T(8,128)(2,1)} %param.14) | copy-start | bytes 1572868
  128.6 52.9 %copy-start.21 = (f32[1,2048]{1,0:T(1,128)S(1)}, f32[1,2048]{1,0:T(1,128)}, u32[]{:S(2)}) copy-start(f32[1,2048]{1,0:T(1,128)} %param.17) | copy-start | bytes 24580
  128.6 3.6 %collective-permute-start.3 = (bf16[32,32,128]{2,1,0:T(8,128)(2,1)S(1)}, bf16[32,32,128]{2,1,0:T(8,128)(2,1)S(1)}, u32[]{:S(2)}, u32[]{:S(2)}) collective-permute-start(bf16[32,32,128]{2,1,0:T(8,128)(2,1)S(1)} %get-tuple-element.21), channel_id=1, source_target_pairs={{0,256},{256,0},{1,257},{257,1},{2,258},{258,2},{3,259},{259,3},{4... | collective-permute-start | bytes 786440 | tf_op jit(solution)/shard_map/ppermute | solution.py:207

commit v2 on v1

v2 whole, which is shorter than its diff:
```python
import math

import jax
import jax.numpy as jnp
import numpy as np
from jax import lax
from jax.experimental import pallas as pl
from jax.experimental.pallas import tpu as pltpu
from jax.sharding import PartitionSpec as P

BF = jnp.bfloat16
F32 = jnp.float32


def angle(rows, cols, modulus):
    product = np.arange(rows)[:, None] * np.arange(cols)[None, :] % modulus
    return product.astype(np.float32) * np.float32(2.0 * math.pi / modulus)


def make_tables(block_rows, local_len, factor):
    half = block_rows // 2
    kept = half + 1
    rows = -(-kept // 16) * 16
    real = (np.arange(rows) < kept).astype(np.float32)[:, None]
    weight = np.where((np.arange(rows) == 0) | (np.arange(rows) == half), 1.0, 2.0)[:, None] * real
    fwd = angle(rows, half, block_rows)
    fwd_rows = np.concatenate([np.cos(fwd) * real, -np.sin(fwd) * real], axis=0)
    back_rows = np.concatenate([np.cos(fwd) * weight, -np.sin(fwd) * weight], axis=0).T * factor
    twid = angle(rows, local_len, block_rows * local_len)
    small = angle(local_len, local_len, local_len)
    c, s = np.cos(small), -np.sin(small)
    mat_fwd = np.block([[c, s], [-s, c]])
    mat_inv = np.block([[c, -s], [s, c]])
    pair = lambda a: np.concatenate([a, a], axis=1)
    return (
        jnp.asarray(fwd_rows, BF),
        jnp.asarray(back_rows, BF),
        jnp.asarray(pair(np.cos(twid)), F32),
        jnp.asarray(pair(-np.sin(twid)), F32),
        jnp.asarray(mat_fwd, BF),
        jnp.asarray(mat_inv, BF),
    )


def dot(a, b):
    return jnp.dot(a, b, preferred_element_type=F32)


def forward(blocks, fwd, tcos, tsin, mat, mixed):
    rows = fwd.shape[0] // 2
    n = blocks[0].shape[-1]
    tc, ts = tcos[...], tsin[...]
    for c in range(0, len(blocks), 2):
        a = dot(fwd[...], jnp.concatenate(blocks[c : c + 2], axis=-1))
        ar, ai = a[:rows], a[rows:]
        re = (ar * tc - ai * ts).astype(BF)
        im = (ar * ts + ai * tc).astype(BF)
        for j in range(2):
            at = pl.ds((c + j) * rows, rows)
            mixed[at, :n] = re[:, j * n : (j + 1) * n]
            mixed[at, n:] = im[:, j * n : (j + 1) * n]
    return dot(mixed[...], mat[...])


def join(re, im):
    return jnp.concatenate([re, im], axis=-1).astype(BF)


def inverse(joined, back, tcos, tsin, mat):
    rows = back.shape[1] // 2
    n = joined.shape[-1] // 2
    tc, ts = tcos[...], tsin[...]
    e = dot(joined, mat[...])
    out = []
    for c in range(0, e.shape[0], 2 * rows):
        e0, e1 = e[c : c + rows], e[c + rows : c + 2 * rows]
        er = jnp.concatenate([e0[:, :n], e1[:, :n]], axis=-1)
        ei = jnp.concatenate([e0[:, n:], e1[:, n:]], axis=-1)
        g = jnp.concatenate([er * tc + ei * ts, ei * tc - er * ts], axis=0).astype(BF)
        o = dot(back[...], g)
        out += [o[:, :n], o[:, n:]]
    return out


def split(spec):
    n = spec.shape[-1] // 2
    return spec[:, :n], spec[:, n:]


def by_channel(a):
    a = jnp.swapaxes(a.astype(F32), 0, 1).astype(BF)
    return [a[c] for c in range(a.shape[0])]


def by_block(parts):
    return jnp.swapaxes(jnp.stack(parts), 0, 1).astype(BF)


def cut_kernel(rows, out):
    out[0] = rows[...]


def pack_kernel(rows, q, k, v, packed, tokens):
    g = rows[...].astype(F32).T
    tokens[...] = g.astype(BF)
    shape = (packed.shape[0],) + packed.shape[2:]
    packed[:, 0] = (k[...].astype(F32) * v[...].astype(F32)).astype(BF).reshape(shape)
    packed[:, 1] = (g * q[...].astype(F32)).astype(BF).reshape(shape)


def filter_kernel(taps, fwd, tc, ts, mf, f_spec, mixed):
    f_spec[...] = forward([taps[c] for c in range(taps.shape[0])], fwd, tc, ts, mf, mixed)


def main_kernel(got, f_spec, fwd, back, tc, ts, mf, mi, both, lag_spec, mixed):
    fr, fi = split(f_spec[...])
    xr, xi = split(forward(by_channel(got[:, 0]), fwd, tc, ts, mf, mixed))
    both[:, 0] = by_block(inverse(join(fr * xr - fi * xi, fr * xi + fi * xr), back, tc, ts, mi))
    gr, gi = split(forward(by_channel(got[:, 1]), fwd, tc, ts, mf, mixed))
    lag_spec[...] = join(xr * gr + xi * gi, xr * gi - xi * gr)
    both[:, 1] = by_block(inverse(join(fr * gr + fi * gi, fr * gi - fi * gr), back, tc, ts, mi))


def out_kernel(both, packed, tokens, k, v, skip, query_out, key_out, value_out):
    shape = tokens.shape
    conv, corr = (both[:, i].astype(F32).reshape(shape) for i in range(2))
    gated, grad = (packed[:, i].astype(F32).reshape(shape) for i in range(2))
    s = skip[...]
    query_out[...] = (tokens[...].astype(F32) * (conv + s * gated)).astype(BF)
    total = corr + s * grad
    key_out[...] = (total * v[...].astype(F32)).astype(BF)
    value_out[...] = (total * k[...].astype(F32)).astype(BF)


def lag_kernel(lag_spec, own_rows, away_rows, tc, ts, mi, own, away):
    rows = own_rows.shape[0]
    both = jnp.concatenate([own_rows[...], away_rows[...]], axis=0)
    parts = inverse(lag_spec[...], both, tc, ts, mi)
    for c, part in enumerate(parts):
        own[c] = part[:rows]
        away[c] = part[rows:].astype(BF)


def call(body, grid, ins, tables, outs, vmem, mixed=None, placed=None):
    hbm = lambda a: a if a is placed else pltpu.with_memory_space_constraint(a, pltpu.HBM)

    def cut(a, dim):
        block = tuple(s // grid if i == dim else s for i, s in enumerate(a.shape))
        return pl.BlockSpec(block, lambda g: tuple(g if i == dim else 0 for i in range(len(block))))

    def whole(a):
        return pl.BlockSpec(a.shape, lambda g: (0,) * len(a.shape))

    return pl.pallas_call(
        body,
        grid=(grid,),
        in_specs=[cut(a, d) for a, d in ins] + [whole(a) for a in tables],
        out_specs=[cut(a, d) for a, d in outs],
        out_shape=[pltpu.HBM(a.shape, a.dtype) for a, _ in outs],
        scratch_shapes=[] if mixed is None else [pltpu.VMEM(mixed, BF)],
        compiler_params=pltpu.CompilerParams(vmem_limit_bytes=vmem * 2**20),
        cost_estimate=pl.CostEstimate(flops=2**20, bytes_accessed=2**20, transcendentals=0),
    )(*[hbm(a) for a, _ in ins], *[hbm(a) for a in tables])


def local(query_proj, key_proj, value_proj, out_grad, filter_taps, skip_gain):
    ctx = lax.axis_size("ctx")
    tp = lax.axis_size("tp")
    dp = lax.axis_size("dp")
    q, k, v = query_proj[0], key_proj[0], value_proj[0]
    chans, block = q.shape
    own = chans // ctx
    factor = 1.0 / (2 * ctx * block)
    fwd, back, tc, ts, mf, mi = make_tables(2 * ctx, block, factor)
    core = lax.axis_index("dp")
    struct = jax.ShapeDtypeStruct
    spec = struct((own * tc.shape[0], 2 * block), F32)
    mixed = (spec.shape[0] // 2, 2 * block)
    packed_type = struct((ctx, 2, own, block), BF)
    chan_type = struct((chans, block), BF)

    def exchange(a):
        flat = a.reshape(ctx, 2 * own, block)
        return lax.all_to_all(flat, "ctx", split_axis=0, concat_axis=0, tiled=True).reshape(a.shape)

    rows = out_grad[0]
    (cuts,) = call(
        cut_kernel, tp, [(rows, 1)], (), [(struct((tp, rows.shape[0], chans), BF), 0)], 16
    )
    rows = lax.all_to_all(cuts, "tp", split_axis=0, concat_axis=0, tiled=True)
    rows = rows.reshape(block, chans)
    packed, tokens = call(
        pack_kernel, 4, [(rows, 1), (q, 0), (k, 0), (v, 0)], (),
        [(packed_type, 0), (chan_type, 0)], 16,
    )
    got = exchange(packed)

    taps = filter_taps[0].reshape(own, ctx, block)
    (f_spec,) = call(filter_kernel, 2, [(taps, 0)], (fwd, tc, ts, mf), [(spec, 0)], 20, mixed)
    both, lag_spec = call(
        main_kernel, 2, [(got, 2), (f_spec, 0)], (fwd, back, tc, ts, mf, mi),
        [(packed_type, 2), (struct(spec.shape, BF), 0)], 32, mixed, got,
    )
    both = exchange(both)

    halves = back.reshape(dp, ctx // dp, -1)
    half_out = (own, ctx // dp, block)
    lag_own, lag_away = call(
        lag_kernel, 2, [(lag_spec, 0)],
        (
            lax.dynamic_index_in_dim(halves, core, keepdims=False),
            lax.dynamic_index_in_dim(halves, lax.rem(core + 1, dp), keepdims=False),
            tc, ts, mi,
        ),
        [(struct(half_out, F32), 0), (struct(half_out, BF), 0)], 28,
    )
    skip = jnp.broadcast_to(skip_gain[0][:, None], (chans, block))
    lag_away, skip = lax.optimization_barrier((lag_away, skip))
    other = lax.ppermute(lag_away, "dp", [(j, (j + 1) % dp) for j in range(dp)])
    grad_scale = 1.0 / math.sqrt(dp * ctx * block)
    filter_out = ((lag_own + other.astype(F32)) * grad_scale).reshape(1, own, -1)

    query_out, key_out, value_out = call(
        out_kernel, 4, [(both, 0), (packed, 0), (tokens, 0), (k, 0), (v, 0), (skip, 0)], (),
        [(chan_type, 0)] * 3, 16, placed=both,
    )
    return (query_out[None], key_out[None], value_out[None], filter_out)


def solution(mesh):
    assert mesh.shape["dp"] == 2
    in_specs = (
        P("dp", "tp", "ctx"),
        P("dp", "tp", "ctx"),
        P("dp", "tp", "ctx"),
        P("dp", ("ctx", "tp"), None),
        P("tp", "ctx", None),
        P("tp", None),
    )
    out_specs = (
        P("dp", "tp", "ctx"),
        P("dp", "tp", "ctx"),
        P("dp", "tp", "ctx"),
        P("tp", "ctx", "dp"),
    )
    return jax.shard_map(local, mesh=mesh, in_specs=in_specs, out_specs=out_specs, check_vma=False)
```

time: 185 us -> 165 us (0.89)
  starting transfers between devices: 52.3 us -> 26.7 us
  local copies, waits for them, and re-layouts: 21.1 us -> 3.74 us
  Pallas kernels: 7.35 us -> 24.3 us
  blocking collectives: 0 us -> 14.1 us
  other arithmetic: 7.7 us -> 1.12 us
    ppermute x3 -> x0, waiting for transfers between devices: 19.9 us -> none  [local(): piece = lax.ppermute(piece, 'tp', [(j, (j + d) % tp) for j in range(tp)])]
    all_to_all x3 -> x2, waiting for transfers between devices: 73.5 us -> 92.3 us  [exchange(): lax.all_to_all(flat, 'ctx', split_axis=0, concat_axis=0, tiled=True)]
    pallas_call x3 -> x6, Pallas kernels: 7.35 us -> 24.3 us  [call(): pl.pallas_call(body, grid=(grid,), in_specs=[cut(a, d) for a, d in ins] +...]
    all_to_all x3 -> x2, starting transfers between devices: 40.1 us -> 24.8 us  [exchange(): lax.all_to_all(flat, 'ctx', split_axis=0, concat_axis=0, tiled=True)]
    all_to_all x0 -> x1, blocking collectives: none -> 14.1 us  [local(): rows = lax.all_to_all(cuts, 'tp', split_axis=0, concat_axis=0, tiled=True)]
    unnamed x45 -> x7, local copies, waits for them, and re-layouts: 11.3 us -> 0.92 us
    ppermute x3 -> x0, starting transfers between devices: 10.2 us -> none  [local(): piece = lax.ppermute(piece, 'tp', [(j, (j + d) % tp) for j in range(tp)])]
    concatenate x1 -> x0, local copies, waits for them, and re-layouts: 5 us -> none  [local(): ring = jnp.concatenate(order, axis=0)]
  transfers between devices with their start and end apart: 7 -> 3, of which waited for: 5 -> 3; matrix products, arithmetic and copies ran while one was open for 6% -> 3% of each run, Pallas kernels for 2% -> 4%
where the time goes in v2:
time: 165 us
  waiting for transfers between devices  94 us (57%)
  starting transfers between devices  26.7 us (16%)
  Pallas kernels  24.3 us (15%)
  blocking collectives  14.1 us (9%)
  local copies, waits for them, and re-layouts  3.74 us (2%)
    all_to_all x2, waiting for transfers between devices, exchange(): lax.all_to_all(flat, 'ctx', split_axis=0, concat_axis=0, tiled=True)  92.3 us
    all_to_all x2, starting transfers between devices, exchange(): lax.all_to_all(flat, 'ctx', split_axis=0, concat_axis=0, tiled=True)  24.8 us
    pallas_call x6, Pallas kernels, call(): pl.pallas_call(body, grid=(grid,), in_specs=[cut(a, d) for a, d in ins] +...  24.3 us
    all_to_all x1, blocking collectives, local(): rows = lax.all_to_all(cuts, 'tp', split_axis=0, concat_axis=0, tiled=True)  14.1 us
  transfers between devices with their start and end apart: 3, of which 3 were waited for; matrix products, arithmetic and copies ran while one was open for 3% of the time, Pallas kernels for 4%

profile of v2, /device:TPU:8, one launch (start us, length us, event | category | flops | bytes accessed | tf_op | source)
XLA Modules:
  0.0 164.8 jit_solution(12067900565215601429)
XLA Ops:
  0.6 3.2 %shard_map.147 = bf16[4,32,2048]{2,1,0:T(8,128)(2,1)} custom-call(bf16[32,8192]{1,0:T(8,128)(2,1)} %bitcast.30), custom_call_target="tpu_custom_call" | custom-call | flops 1048576 | bytes 1048576 | tf_op jit(solution)/shard_map/pallas_call | solution.py:154
  3.8 0.0 copy-start
  3.8 14.1 %all_to_all.15 = bf16[4,32,2048]{2,1,0:T(8,128)(2,1)} all-to-all(bf16[4,32,2048]{2,1,0:T(8,128)(2,1)} %shard_map.147), channel_id=1, replica_groups=mesh['dp'=2,'ctx'=64,'tp'=4] {'tp'}, dimensions={0} | all-to-all | bytes 1048576 | tf_op jit(solution)/shard_map/all_to_all | solution.py:190
  17.9 3.9 %shard_map.148 = (bf16[64,2,32,128]{3,2,1,0:T(8,128)(2,1)}, bf16[2048,128]{1,0:T(8,128)(2,1)}) custom-call(bf16[128,2048]{1,0:T(8,128)(2,1)} %bitcast.27, bf16[2048,128]{1,0:T(8,128)(2,1)} %bitcast.32, bf16[2048,128]{1,0:T(8,128)(2,1)} %bitcast.23, bf16[2048,128]{1,0:T(8,128)(2,1)} %bitcast.25), custom_call_target="tpu_custom_call" | custom-call | flops 1048576 | bytes 1048576 | tf_op jit(solution)/shard_map/pallas_call | solution.py:154
  21.8 18.7 %all-to-all-start.1 = ((bf16[64,64,128]{2,1,0:T(8,128)(2,1)}), bf16[64,64,128]{2,1,0:T(8,128)(2,1)S(1)}, u32[]{:S(2)}, u32[]{:S(2)}) async-start(bf16[64,64,128]{2,1,0:T(8,128)(2,1)} %bitcast.22), calls=%async_computation.1 | async-start | bytes 2097152 | tf_op jit(solution)/shard_map/all_to_all | solution.py:184
  40.6 0.0 copy-done
  40.6 0.9 copy.16
  41.5 3.4 %shard_map.149.f_spec = f32[2560,256]{1,0:T(8,128)} custom-call(bf16[32,64,128]{2,1,0:T(8,128)(2,1)} %bitcast.28, bf16[160,64]{1,0:T(8,128)(2,1)} %constant.33.clone.fwd, f32[80,256]{1,0:T(8,128)} %constant.35.clone.tc, f32[80,256]{1,0:T(8,128)} %constant.36.clone.ts, bf16[256,256]{1,0:T(8,128)(2,1)} %constant.37.clone.mf), custom_call_target="tpu_custom_call" | custom-call | flops 1048576 | bytes 1048576 | tf_op jit(solution)/shard_map/pallas_call | solution.py:154
  44.9 49.7 %all-to-all-done.1 = bf16[64,64,128]{2,1,0:T(8,128)(2,1)S(1)} async-done(((bf16[64,64,128]{2,1,0:T(8,128)(2,1)}), bf16[64,64,128]{2,1,0:T(8,128)(2,1)S(1)}, u32[]{:S(2)}, u32[]{:S(2)}) %all-to-all-start.1) | async-done | bytes 1048608 | tf_op jit(solution)/shard_map/all_to_all | solution.py:184
  94.6 0.0 copy-start.1
  94.6 6.7 %shard_map.150 = (bf16[64,2,32,128]{3,2,1,0:T(8,128)(2,1)}, bf16[2560,256]{1,0:T(8,128)(2,1)}) custom-call(bf16[64,2,32,128]{3,2,1,0:T(8,128)(2,1)S(1)} %bitcast.21, f32[2560,256]{1,0:T(8,128)} %shard_map.149.f_spec, bf16[160,64]{1,0:T(8,128)(2,1)} %constant.33.clone.fwd, bf16[64,160]{1,0:T(8,128)(2,1)} %constant.34.clone.back, ...), custom_call_target="tpu_custom_call" | custom-call | flops 1048576 | bytes 1048576 | tf_op jit(solution)/shard_map/pallas_call | solution.py:154
  101.2 0.0 copy-start.2
  101.3 6.1 %all-to-all-start.2 = ((bf16[64,64,128]{2,1,0:T(8,128)(2,1)}), bf16[64,64,128]{2,1,0:T(8,128)(2,1)S(1)}, u32[]{:S(2)}, u32[]{:S(2)}) async-start(bf16[64,64,128]{2,1,0:T(8,128)(2,1)} %bitcast.29), calls=%async_computation.2 | async-start | bytes 2097152 | tf_op jit(solution)/shard_map/all_to_all | solution.py:184
  107.3 0.0 copy-done.1
  107.4 0.6 dynamic-slice_bitcast_fusion
  108.0 3.2 %shard_map.151 = (f32[32,32,128]{2,1,0:T(8,128)}, bf16[32,32,128]{2,1,0:T(8,128)(2,1)}) custom-call(bf16[2560,256]{1,0:T(8,128)(2,1)} %get-tuple-element.18.lag_spec, bf16[32,160]{1,0:T(8,128)(2,1)} %get-tuple-element.27.own_rows, bf16[32,160]{1,0:T(8,128)(2,1)} %get-tuple-element.26.away_rows, f32[80,256]{1,0:T(8,128)} %constant.35.clone.tc, ...), custom_call_target="tpu_custom_call" | custom-call | flops 1048576 | bytes 1048576 | tf_op jit(solution)/shard_map/pallas_call | solution.py:154
  111.1 0.0 copy-done.2
  111.2 1.3 broadcast_in_dim.17.skip
  112.5 1.9 %collective-permute-start = (bf16[32,32,128]{2,1,0:T(8,128)(2,1)}, bf16[32,32,128]{2,1,0:T(8,128)(2,1)S(1)}, u32[]{:S(2)}, u32[]{:S(2)}) collective-permute-start(bf16[32,32,128]{2,1,0:T(8,128)(2,1)} %get-tuple-element.25), channel_id=1, source_target_pairs={{0,256},{256,0},{1,257},{257,1},{2,258},{258,2},{3,259},{259,3},{4... | collective-permute-start | bytes 786440 | tf_op jit(solution)/shard_map/ppermute | solution.py:219
  114.4 1.7 %collective-permute-done = bf16[32,32,128]{2,1,0:T(8,128)(2,1)S(1)} collective-permute-done((bf16[32,32,128]{2,1,0:T(8,128)(2,1)}, bf16[32,32,128]{2,1,0:T(8,128)(2,1)S(1)}, u32[]{:S(2)}, u32[]{:S(2)}) %collective-permute-start) | collective-permute-done | bytes 262176 | tf_op jit(solution)/shard_map/ppermute | solution.py:219
  116.1 1.1 add_multiply_fusion
  117.2 0.9 reshape.36
  118.1 42.6 %all-to-all-done.2 = bf16[64,64,128]{2,1,0:T(8,128)(2,1)S(1)} async-done(((bf16[64,64,128]{2,1,0:T(8,128)(2,1)}), bf16[64,64,128]{2,1,0:T(8,128)(2,1)S(1)}, u32[]{:S(2)}, u32[]{:S(2)}) %all-to-all-start.2) | async-done | bytes 1048608 | tf_op jit(solution)/shard_map/all_to_all | solution.py:184
  160.7 4.0 %shard_map.152 = (bf16[2048,128]{1,0:T(8,128)(2,1)}, bf16[2048,128]{1,0:T(8,128)(2,1)}, bf16[2048,128]{1,0:T(8,128)(2,1)}) custom-call(bf16[64,2,32,128]{3,2,1,0:T(8,128)(2,1)S(1)} %bitcast.20, bf16[64,2,32,128]{3,2,1,0:T(8,128)(2,1)} %get-tuple-element.15.packed, bf16[2048,128]{1,0:T(8,128)(2,1)} %get-tuple-element.17.tokens, bf16[2048,128]{1,0:T(8,128)(2,1)} %bitcast.24, ...), custom_call_target="tpu_custom_call" | custom-call | flops 1048576 | bytes 1048576 | tf_op jit(solution)/shard_map/pallas_call | solution.py:154
Async XLA Ops:
  3.8 36.8 %copy-start = (bf16[1,32,8192]{2,1,0:T(8,128)(2,1)S(1)}, bf16[1,32,8192]{2,1,0:T(8,128)(2,1)}, u32[]{:S(2)}) copy-start(bf16[1,32,8192]{2,1,0:T(8,128)(2,1)} %param.16) | copy-start | bytes 1572868
  21.8 72.7 %all-to-all-start.1 = ((bf16[64,64,128]{2,1,0:T(8,128)(2,1)}), bf16[64,64,128]{2,1,0:T(8,128)(2,1)S(1)}, u32[]{:S(2)}, u32[]{:S(2)}) async-start(bf16[64,64,128]{2,1,0:T(8,128)(2,1)} %bitcast.22), calls=%async_computation.1 | async-start | bytes 2097152 | tf_op jit(solution)/shard_map/all_to_all | solution.py:184
  94.6 12.8 %copy-start.1 = (bf16[2,32,160]{2,1,0:T(8,128)(2,1)S(1)}, bf16[2,32,160]{2,1,0:T(8,128)(2,1)}, u32[]{:S(2)}) copy-start(bf16[2,32,160]{2,1,0:T(8,128)(2,1)} %constant.45) | copy-start | bytes 61444
  101.2 9.9 %copy-start.2 = (f32[1,2048]{1,0:T(1,128)S(1)}, f32[1,2048]{1,0:T(1,128)}, u32[]{:S(2)}) copy-start(f32[1,2048]{1,0:T(1,128)} %param.17) | copy-start | bytes 24580
  101.3 59.5 %all-to-all-start.2 = ((bf16[64,64,128]{2,1,0:T(8,128)(2,1)}), bf16[64,64,128]{2,1,0:T(8,128)(2,1)S(1)}, u32[]{:S(2)}, u32[]{:S(2)}) async-start(bf16[64,64,128]{2,1,0:T(8,128)(2,1)} %bitcast.29), calls=%async_computation.2 | async-start | bytes 2097152 | tf_op jit(solution)/shard_map/all_to_all | solution.py:184
  112.5 3.6 %collective-permute-start = (bf16[32,32,128]{2,1,0:T(8,128)(2,1)}, bf16[32,32,128]{2,1,0:T(8,128)(2,1)S(1)}, u32[]{:S(2)}, u32[]{:S(2)}) collective-permute-start(bf16[32,32,128]{2,1,0:T(8,128)(2,1)} %get-tuple-element.25), channel_id=1, source_target_pairs={{0,256},{256,0},{1,257},{257,1},{2,258},{258,2},{3,259},{259,3},{4... | collective-permute-start | bytes 786440 | tf_op jit(solution)/shard_map/ppermute | solution.py:219

commit v3 on v2

--- a/solution.py
+++ b/solution.py
@@ -96,16 +96,30 @@
     return jnp.swapaxes(jnp.stack(parts), 0, 1).astype(BF)
 
 
-def cut_kernel(rows, out):
-    out[0] = rows[...]
-
-
-def pack_kernel(rows, q, k, v, packed, tokens):
-    g = rows[...].astype(F32).T
-    tokens[...] = g.astype(BF)
+def cut_kernel(rows, out, sems):
+    width = out.shape[2]
+    copies = [
+        pltpu.make_async_copy(rows.at[:, pl.ds(i * width, width)], out.at[i], sems.at[i])
+        for i in range(out.shape[0])
+    ]
+    for copy in copies:
+        copy.start()
+    for copy in copies:
+        copy.wait()
+
+
+def gated_kernel(k, v, packed):
     shape = (packed.shape[0],) + packed.shape[2:]
     packed[:, 0] = (k[...].astype(F32) * v[...].astype(F32)).astype(BF).reshape(shape)
-    packed[:, 1] = (g * q[...].astype(F32)).astype(BF).reshape(shape)
+
+
+def grad_kernel(rows, q, half_packed, packed):
+    shape = (packed.shape[0],) + packed.shape[2:]
+    packed[:, 0] = (rows[...].astype(F32).T * q[...].astype(F32)).astype(BF).reshape(shape)
+
+
+def tokens_kernel(rows, tokens):
+    tokens[...] = rows[...].astype(F32).T.astype(BF)
 
 
 def filter_kernel(taps, fwd, tc, ts, mf, f_spec, mixed):
@@ -123,11 +137,12 @@
 
 def out_kernel(both, packed, tokens, k, v, skip, query_out, key_out, value_out):
     shape = tokens.shape
-    conv, corr = (both[:, i].astype(F32).reshape(shape) for i in range(2))
-    gated, grad = (packed[:, i].astype(F32).reshape(shape) for i in range(2))
-    s = skip[...]
-    query_out[...] = (tokens[...].astype(F32) * (conv + s * gated)).astype(BF)
-    total = corr + s * grad
+    s = lax.broadcast_in_dim(skip[...], skip.shape + (shape[1],), (0, 1))
+    conv, corr = (both[:, i].astype(F32) for i in range(2))
+    gated, grad = (packed[:, i].astype(F32) for i in range(2))
+    through = (conv + s * gated).reshape(shape)
+    query_out[...] = (tokens[...].astype(F32) * through).astype(BF)
+    total = (corr + s * grad).reshape(shape)
     key_out[...] = (total * v[...].astype(F32)).astype(BF)
     value_out[...] = (total * k[...].astype(F32)).astype(BF)
 
@@ -141,26 +156,35 @@
         away[c] = part[rows:].astype(BF)
 
 
-def call(body, grid, ins, tables, outs, vmem, mixed=None, placed=None):
-    hbm = lambda a: a if a is placed else pltpu.with_memory_space_constraint(a, pltpu.HBM)
-
-    def cut(a, dim):
-        block = tuple(s // grid if i == dim else s for i, s in enumerate(a.shape))
-        return pl.BlockSpec(block, lambda g: tuple(g if i == dim else 0 for i in range(len(block))))
-
-    def whole(a):
-        return pl.BlockSpec(a.shape, lambda g: (0,) * len(a.shape))
-
+def hbm(a):
+    return pltpu.with_memory_space_constraint(a, pltpu.HBM)
+
+
+def hbm_out(a):
+    return pltpu.HBM(a.shape, a.dtype)
+
+
+def cut(a, dim, grid, at=None):
+    block = [s // grid if i == dim else s for i, s in enumerate(a.shape)]
+    index = [0] * len(block)
+    if at:
+        block[at[0]], index[at[0]] = 1, at[1]
+    return pl.BlockSpec(
+        tuple(block), lambda g: tuple(g if i == dim else n for i, n in enumerate(index))
+    )
+
+
+def call(body, grid, ins, tables, outs, vmem, mixed=None):
     return pl.pallas_call(
         body,
         grid=(grid,),
-        in_specs=[cut(a, d) for a, d in ins] + [whole(a) for a in tables],
-        out_specs=[cut(a, d) for a, d in outs],
-        out_shape=[pltpu.HBM(a.shape, a.dtype) for a, _ in outs],
+        in_specs=[cut(a, d, grid) for a, d in ins] + [cut(a, None, grid) for a in tables],
+        out_specs=[cut(a, d, grid) for a, d in outs],
+        out_shape=[a for a, _ in outs],
         scratch_shapes=[] if mixed is None else [pltpu.VMEM(mixed, BF)],
         compiler_params=pltpu.CompilerParams(vmem_limit_bytes=vmem * 2**20),
         cost_estimate=pl.CostEstimate(flops=2**20, bytes_accessed=2**20, transcendentals=0),
-    )(*[hbm(a) for a, _ in ins], *[hbm(a) for a in tables])
+    )(*[a for a, _ in ins], *[hbm(a) for a in tables])
 
 
 def local(query_proj, key_proj, value_proj, out_grad, filter_taps, skip_gain):
@@ -184,22 +208,44 @@
         return lax.all_to_all(flat, "ctx", split_axis=0, concat_axis=0, tiled=True).reshape(a.shape)
 
     rows = out_grad[0]
-    (cuts,) = call(
-        cut_kernel, tp, [(rows, 1)], (), [(struct((tp, rows.shape[0], chans), BF), 0)], 16
-    )
+    anywhere = pl.BlockSpec(memory_space=pl.ANY)
+    cuts = pl.pallas_call(
+        cut_kernel,
+        in_specs=[anywhere],
+        out_specs=anywhere,
+        out_shape=pltpu.HBM((tp, rows.shape[0], chans), BF),
+        scratch_shapes=[pltpu.SemaphoreType.DMA((tp,))],
+    )(hbm(rows))
     rows = lax.all_to_all(cuts, "tp", split_axis=0, concat_axis=0, tiled=True)
     rows = rows.reshape(block, chans)
-    packed, tokens = call(
-        pack_kernel, 4, [(rows, 1), (q, 0), (k, 0), (v, 0)], (),
-        [(packed_type, 0), (chan_type, 0)], 16,
-    )
+
+    grid = 4
+    params = pltpu.CompilerParams(vmem_limit_bytes=16 * 2**20)
+    half_packed = pl.pallas_call(
+        gated_kernel,
+        grid=(grid,),
+        in_specs=[cut(k, 0, grid), cut(v, 0, grid)],
+        out_specs=cut(packed_type, 0, grid, (1, 0)),
+        out_shape=hbm_out(packed_type),
+        compiler_params=params,
+    )(hbm(k), hbm(v))
+    packed = pl.pallas_call(
+        grad_kernel,
+        grid=(grid,),
+        in_specs=[cut(rows, 1, grid), cut(q, 0, grid), anywhere],
+        out_specs=cut(packed_type, 0, grid, (1, 1)),
+        out_shape=hbm_out(packed_type),
+        input_output_aliases={2: 0},
+        compiler_params=params,
+    )(rows, hbm(q), hbm(half_packed))
+    (tokens,) = call(tokens_kernel, grid, [(rows, 1)], (), [(hbm_out(chan_type), 0)], 16)
     got = exchange(packed)
 
     taps = filter_taps[0].reshape(own, ctx, block)
     (f_spec,) = call(filter_kernel, 2, [(taps, 0)], (fwd, tc, ts, mf), [(spec, 0)], 20, mixed)
     both, lag_spec = call(
         main_kernel, 2, [(got, 2), (f_spec, 0)], (fwd, back, tc, ts, mf, mi),
-        [(packed_type, 2), (struct(spec.shape, BF), 0)], 32, mixed, got,
+        [(hbm_out(packed_type), 2), (hbm_out(struct(spec.shape, BF)), 0)], 32, mixed,
     )
     both = exchange(both)
 
@@ -214,15 +260,14 @@
         ),
         [(struct(half_out, F32), 0), (struct(half_out, BF), 0)], 28,
     )
-    skip = jnp.broadcast_to(skip_gain[0][:, None], (chans, block))
-    lag_away, skip = lax.optimization_barrier((lag_away, skip))
     other = lax.ppermute(lag_away, "dp", [(j, (j + 1) % dp) for j in range(dp)])
     grad_scale = 1.0 / math.sqrt(dp * ctx * block)
     filter_out = ((lag_own + other.astype(F32)) * grad_scale).reshape(1, own, -1)
 
     query_out, key_out, value_out = call(
-        out_kernel, 4, [(both, 0), (packed, 0), (tokens, 0), (k, 0), (v, 0), (skip, 0)], (),
-        [(chan_type, 0)] * 3, 16, placed=both,
+        out_kernel, grid,
+        [(both, 0), (packed, 0), (tokens, 0), (hbm(k), 0), (hbm(v), 0), (skip_gain[0].reshape(ctx, own), 0)],
+        (), [(hbm_out(chan_type), 0)] * 3, 16,
     )
     return (query_out[None], key_out[None], value_out[None], filter_out)
 

time: 165 us -> 178 us (1.079)
  Pallas kernels: 24.3 us -> 40.4 us
  blocking collectives: 14.1 us -> 0 us
  starting transfers between devices: 26.7 us -> 31.2 us
  waiting for transfers between devices: 94 us -> 97.7 us
    pallas_call x6 -> x8, Pallas kernels: 24.3 us -> 40.4 us  [the longest x1 17 us: local(): pl.pallas_call(cut_kernel, in_specs=[anywhere], out_specs=anywhere, out_s...]
    all_to_all x1 -> x0, blocking collectives: 14.1 us -> none  [local(): rows = lax.all_to_all(cuts, 'tp', split_axis=0, concat_axis=0, tiled=True)]
    all_to_all x0 -> x1, waiting for transfers between devices: none -> 6.11 us  [local(): rows = lax.all_to_all(cuts, 'tp', split_axis=0, concat_axis=0, tiled=True)]
    all_to_all x0 -> x1, starting transfers between devices: none -> 4.3 us  [local(): rows = lax.all_to_all(cuts, 'tp', split_axis=0, concat_axis=0, tiled=True)]
  transfers between devices with their start and end apart: 3 -> 4, of which waited for: 3 -> 3; matrix products, arithmetic and copies ran while one was open for 3% -> 3% of each run, Pallas kernels for 4% -> 5%
where the time goes in v3:
time: 178 us; the launch traced here: 177 us
  waiting for transfers between devices  97.7 us (55%)
  Pallas kernels  40.4 us (23%)
  starting transfers between devices  31.2 us (18%)
  local copies, waits for them, and re-layouts  4.59 us (3%)
  other arithmetic  2.54 us (1%)
    all_to_all x2, waiting for transfers between devices, exchange(): lax.all_to_all(flat, 'ctx', split_axis=0, concat_axis=0, tiled=True)  91.6 us
    all_to_all x2, starting transfers between devices, exchange(): lax.all_to_all(flat, 'ctx', split_axis=0, concat_axis=0, tiled=True)  25 us
    pallas_call x1, Pallas kernels, local(): pl.pallas_call(cut_kernel, in_specs=[anywhere], out_specs=anywhere, out_s...  17 us
    pallas_call x5, Pallas kernels, call(): pl.pallas_call(body, grid=(grid,), in_specs=[cut(a, d, grid) for a, d in...  16.5 us
    all_to_all x1, waiting for transfers between devices, local(): rows = lax.all_to_all(cuts, 'tp', split_axis=0, concat_axis=0, tiled=True)  6.11 us
    all_to_all x1, starting transfers between devices, local(): rows = lax.all_to_all(cuts, 'tp', split_axis=0, concat_axis=0, tiled=True)  4.3 us
  transfers between devices with their start and end apart: 4, of which 3 were waited for; matrix products, arithmetic and copies ran while one was open for 3% of the time, Pallas kernels for 5%

profile of v3, /device:TPU:8, one launch (start us, length us, event | category | flops | bytes accessed | tf_op | source)
XLA Modules:
  0.0 177.2 jit_solution(1641189323819688910)
XLA Ops:
  0.6 17.0 %shard_map.147 = bf16[4,32,2048]{2,1,0:T(8,128)(2,1)} custom-call(bf16[32,8192]{1,0:T(8,128)(2,1)} %bitcast.29), custom_call_target="tpu_custom_call" | custom-call | tf_op jit(solution)/shard_map/pallas_call | solution.py:212
  17.7 4.3 %all-to-all-start = ((bf16[4,32,2048]{2,1,0:T(8,128)(2,1)}), bf16[4,32,2048]{2,1,0:T(8,128)(2,1)S(1)}, u32[]{:S(2)}, u32[]{:S(2)}) async-start(bf16[4,32,2048]{2,1,0:T(8,128)(2,1)} %shard_map.147), calls=%async_computation | async-start | bytes 1048576 | tf_op jit(solution)/shard_map/all_to_all | solution.py:219
  22.0 3.4 %shard_map.148.half_packed = bf16[64,2,32,128]{3,2,1,0:T(8,128)(2,1)} custom-call(bf16[2048,128]{1,0:T(8,128)(2,1)} %bitcast.24, bf16[2048,128]{1,0:T(8,128)(2,1)} %bitcast.26), custom_call_target="tpu_custom_call" | custom-call | tf_op jit(solution)/shard_map/pallas_call | solution.py:224
  25.3 6.1 %all-to-all-done = bf16[4,32,2048]{2,1,0:T(8,128)(2,1)S(1)} async-done(((bf16[4,32,2048]{2,1,0:T(8,128)(2,1)}), bf16[4,32,2048]{2,1,0:T(8,128)(2,1)S(1)}, u32[]{:S(2)}, u32[]{:S(2)}) %all-to-all-start) | async-done | bytes 524320 | tf_op jit(solution)/shard_map/all_to_all | solution.py:219
  31.4 0.0 copy-start.3
  31.4 3.5 %shard_map.149.packed = bf16[64,2,32,128]{3,2,1,0:T(8,128)(2,1)} custom-call(bf16[128,2048]{1,0:T(8,128)(2,1)S(1)} %bitcast.20, bf16[2048,128]{1,0:T(8,128)(2,1)} %bitcast.31, bf16[64,2,32,128]{3,2,1,0:T(8,128)(2,1)} %shard_map.148.half_packed), custom_call_target="tpu_custom_call", output_to_operand_aliasing={{}: (2, {})} | custom-call | tf_op jit(solution)/shard_map/pallas_call | solution.py:232
  34.9 18.9 %all-to-all-start.1 = ((bf16[64,64,128]{2,1,0:T(8,128)(2,1)}), bf16[64,64,128]{2,1,0:T(8,128)(2,1)}, u32[]{:S(2)}, u32[]{:S(2)}) async-start(bf16[64,64,128]{2,1,0:T(8,128)(2,1)} %bitcast.19), calls=%async_computation.1 | async-start | bytes 2097152 | tf_op jit(solution)/shard_map/all_to_all | solution.py:208
  53.8 0.0 copy-done.3
  53.8 0.1 copy.17
  54.0 2.2 %shard_map.150.f_spec = f32[2560,256]{1,0:T(8,128)S(1)} custom-call(bf16[32,64,128]{2,1,0:T(8,128)(2,1)S(1)} %bitcast.23, bf16[160,64]{1,0:T(8,128)(2,1)} %constant.33.clone.fwd, f32[80,256]{1,0:T(8,128)} %constant.35.clone.tc, f32[80,256]{1,0:T(8,128)} %constant.36.clone.ts, bf16[256,256]{1,0:T(8,128)(2,1)} %constant.37.clone.mf), custom_call_target="tpu_custom_call" | custom-call | flops 1048576 | bytes 1048576 | tf_op jit(solution)/shard_map/pallas_call | solution.py:178
  56.2 51.2 %all-to-all-done.1 = bf16[64,64,128]{2,1,0:T(8,128)(2,1)} async-done(((bf16[64,64,128]{2,1,0:T(8,128)(2,1)}), bf16[64,64,128]{2,1,0:T(8,128)(2,1)}, u32[]{:S(2)}, u32[]{:S(2)}) %all-to-all-start.1) | async-done | bytes 1048608 | tf_op jit(solution)/shard_map/all_to_all | solution.py:208
  107.4 0.0 copy-start.4
  107.4 6.5 %shard_map.151 = (bf16[64,2,32,128]{3,2,1,0:T(8,128)(2,1)}, bf16[2560,256]{1,0:T(8,128)(2,1)}) custom-call(bf16[64,2,32,128]{3,2,1,0:T(8,128)(2,1)} %bitcast.6.got, f32[2560,256]{1,0:T(8,128)S(1)} %shard_map.150.f_spec, bf16[160,64]{1,0:T(8,128)(2,1)} %constant.33.clone.fwd, bf16[64,160]{1,0:T(8,128)(2,1)} %constant.34.clone.back, ...), custom_call_target="tpu_custom_call" | custom-call | flops 1048576 | bytes 1048576 | tf_op jit(solution)/shard_map/pallas_call | solution.py:178
  113.9 0.0 copy-start.5
  113.9 6.1 %all-to-all-start.2 = ((bf16[64,64,128]{2,1,0:T(8,128)(2,1)}), bf16[64,64,128]{2,1,0:T(8,128)(2,1)S(1)}, u32[]{:S(2)}, u32[]{:S(2)}) async-start(bf16[64,64,128]{2,1,0:T(8,128)(2,1)} %bitcast.28), calls=%async_computation.2 | async-start | bytes 2097152 | tf_op jit(solution)/shard_map/all_to_all | solution.py:208
  120.0 0.0 copy-start
  120.0 0.0 copy-done.4
  120.0 0.6 dynamic-slice_bitcast_fusion
  120.6 0.0 copy-start.2
  120.6 1.3 copy-done.2
  121.9 2.3 %shard_map.154 = (f32[32,32,128]{2,1,0:T(8,128)S(1)}, bf16[32,32,128]{2,1,0:T(8,128)(2,1)S(1)}) custom-call(bf16[2560,256]{1,0:T(8,128)(2,1)S(1)} %copy-done.2, bf16[32,160]{1,0:T(8,128)(2,1)} %get-tuple-element.19.own_rows, bf16[32,160]{1,0:T(8,128)(2,1)} %get-tuple-element.18.away_rows, f32[80,256]{1,0:T(8,128)} %constant.35.clone.tc, ...), custom_call_target="tpu_custom_call" | custom-call | flops 1048576 | bytes 1048576 | tf_op jit(solution)/shard_map/pallas_call | solution.py:178
  124.2 1.9 %collective-permute-start = (bf16[32,32,128]{2,1,0:T(8,128)(2,1)S(1)}, bf16[32,32,128]{2,1,0:T(8,128)(2,1)}, u32[]{:S(2)}, u32[]{:S(2)}) collective-permute-start(bf16[32,32,128]{2,1,0:T(8,128)(2,1)S(1)} %get-tuple-element.17), channel_id=1, source_target_pairs={{0,256},{256,0},{1,257},{257,1},{2,258},{258,2},{3,259},{259,3},{4... | collective-permute-start | bytes 786440 | tf_op jit(solution)/shard_map/ppermute | solution.py:263
  126.2 0.5 broadcast.4
  126.7 0.0 copy-done.5
  126.7 0.7 reduce.3
  127.3 0.1 reshape_squeeze.7.skip
  127.4 1.7 shard_map.152.tokens
  129.1 0.0 copy-start.1
  129.1 0.0 collective-permute-done
  129.1 1.9 %add_multiply_fusion = f32[32,32,128]{2,1,0:T(8,128)} fusion(f32[32,32,128]{2,1,0:T(8,128)S(1)} %get-tuple-element.16, bf16[32,32,128]{2,1,0:T(8,128)(2,1)} %collective-permute-done), kind=kLoop, calls=%fused_computation | loop fusion | flops 393216 | bytes 1310720 | tf_op jit(solution)/shard_map/mul | solution.py:265
  131.0 1.9 %reshape.35 = f32[1,32,4096]{2,1,0:T(8,128)} reshape(f32[32,32,128]{2,1,0:T(8,128)} %add_multiply_fusion) | data formatting | bytes 1048576 | tf_op jit(solution)/shard_map/reshape | solution.py:265
  132.9 40.4 %all-to-all-done.2 = bf16[64,64,128]{2,1,0:T(8,128)(2,1)S(1)} async-done(((bf16[64,64,128]{2,1,0:T(8,128)(2,1)}), bf16[64,64,128]{2,1,0:T(8,128)(2,1)S(1)}, u32[]{:S(2)}, u32[]{:S(2)}) %all-to-all-start.2) | async-done | bytes 1048608 | tf_op jit(solution)/shard_map/all_to_all | solution.py:208
  173.3 0.0 copy-done
  173.3 0.0 copy-done.1
  173.3 3.9 %shard_map.153 = (bf16[2048,128]{1,0:T(8,128)(2,1)}, bf16[2048,128]{1,0:T(8,128)(2,1)}, bf16[2048,128]{1,0:T(8,128)(2,1)}) custom-call(bf16[64,2,32,128]{3,2,1,0:T(8,128)(2,1)S(1)} %bitcast.22, bf16[64,2,32,128]{3,2,1,0:T(8,128)(2,1)S(1)} %copy-done, bf16[2048,128]{1,0:T(8,128)(2,1)S(1)} %copy-done.1, bf16[2048,128]{1,0:T(8,128)(2,1)} %bitcast.25, ...), custom_call_target="tpu_custom_call" | custom-call | flops 1048576 | bytes 1048576 | tf_op jit(solution)/shard_map/pallas_call | solution.py:178
Async XLA Ops:
  17.7 13.8 %all-to-all-start = ((bf16[4,32,2048]{2,1,0:T(8,128)(2,1)}), bf16[4,32,2048]{2,1,0:T(8,128)(2,1)S(1)}, u32[]{:S(2)}, u32[]{:S(2)}) async-start(bf16[4,32,2048]{2,1,0:T(8,128)(2,1)} %shard_map.147), calls=%async_computation | async-start | bytes 1048576 | tf_op jit(solution)/shard_map/all_to_all | solution.py:219
  31.4 22.4 %copy-start.3 = (bf16[1,32,8192]{2,1,0:T(8,128)(2,1)S(1)}, bf16[1,32,8192]{2,1,0:T(8,128)(2,1)}, u32[]{:S(2)}) copy-start(bf16[1,32,8192]{2,1,0:T(8,128)(2,1)} %param.16) | copy-start | bytes 1572868
  34.9 72.5 %all-to-all-start.1 = ((bf16[64,64,128]{2,1,0:T(8,128)(2,1)}), bf16[64,64,128]{2,1,0:T(8,128)(2,1)}, u32[]{:S(2)}, u32[]{:S(2)}) async-start(bf16[64,64,128]{2,1,0:T(8,128)(2,1)} %bitcast.19), calls=%async_computation.1 | async-start | bytes 2097152 | tf_op jit(solution)/shard_map/all_to_all | solution.py:208
  107.4 12.6 %copy-start.4 = (bf16[2,32,160]{2,1,0:T(8,128)(2,1)S(1)}, bf16[2,32,160]{2,1,0:T(8,128)(2,1)}, u32[]{:S(2)}) copy-start(bf16[2,32,160]{2,1,0:T(8,128)(2,1)} %constant.45) | copy-start | bytes 61444
  113.9 12.8 %copy-start.5 = (f32[1,2048]{1,0:T(1,128)S(1)}, f32[1,2048]{1,0:T(1,128)}, u32[]{:S(2)}) copy-start(f32[1,2048]{1,0:T(1,128)} %param.17) | copy-start | bytes 24580
  113.9 59.4 %all-to-all-start.2 = ((bf16[64,64,128]{2,1,0:T(8,128)(2,1)}), bf16[64,64,128]{2,1,0:T(8,128)(2,1)S(1)}, u32[]{:S(2)}, u32[]{:S(2)}) async-start(bf16[64,64,128]{2,1,0:T(8,128)(2,1)} %bitcast.28), calls=%async_computation.2 | async-start | bytes 2097152 | tf_op jit(solution)/shard_map/all_to_all | solution.py:208
  120.0 53.3 %copy-start = (bf16[64,2,32,128]{3,2,1,0:T(8,128)(2,1)S(1)}, bf16[64,2,32,128]{3,2,1,0:T(8,128)(2,1)}, u32[]{:S(2)}) copy-start(bf16[64,2,32,128]{3,2,1,0:T(8,128)(2,1)} %shard_map.149.packed) | copy-start | bytes 3145732
  120.6 1.3 copy-start.2
  124.2 4.9 %collective-permute-start = (bf16[32,32,128]{2,1,0:T(8,128)(2,1)S(1)}, bf16[32,32,128]{2,1,0:T(8,128)(2,1)}, u32[]{:S(2)}, u32[]{:S(2)}) collective-permute-start(bf16[32,32,128]{2,1,0:T(8,128)(2,1)S(1)} %get-tuple-element.17), channel_id=1, source_target_pairs={{0,256},{256,0},{1,257},{257,1},{2,258},{258,2},{3,259},{259,3},{4... | collective-permute-start | bytes 786440 | tf_op jit(solution)/shard_map/ppermute | solution.py:263
  129.1 44.2 %copy-start.1 = (bf16[2048,128]{1,0:T(8,128)(2,1)S(1)}, bf16[2048,128]{1,0:T(8,128)(2,1)}, u32[]{:S(2)}) copy-start(bf16[2048,128]{1,0:T(8,128)(2,1)} %shard_map.152.tokens) | copy-start | bytes 1572868

commit v4 on v3

--- a/solution.py
+++ b/solution.py
@@ -1,3 +1,4 @@
+import functools
 import math
 
 import jax
@@ -96,19 +97,30 @@
     return jnp.swapaxes(jnp.stack(parts), 0, 1).astype(BF)
 
 
-def cut_kernel(rows, out, sems):
-    width = out.shape[2]
-    copies = [
-        pltpu.make_async_copy(rows.at[:, pl.ds(i * width, width)], out.at[i], sems.at[i])
-        for i in range(out.shape[0])
-    ]
-    for copy in copies:
+def cut_kernel(rows, out, held, sems):
+    parts, count, width = out.shape
+    half = count // 2
+    ins, outs = [], []
+    for i in range(parts):
+        for j in range(2):
+            at = pl.ds(j * half, half)
+            n = 2 * i + j
+            here = held.at[i, at]
+            ins.append(
+                pltpu.make_async_copy(rows.at[at, pl.ds(i * width, width)], here, sems.at[0, n])
+            )
+            outs.append(pltpu.make_async_copy(here, out.at[i, at], sems.at[1, n]))
+    for copy in ins:
         copy.start()
-    for copy in copies:
+    for copy, back in zip(ins, outs):
         copy.wait()
-
-
-def gated_kernel(k, v, packed):
+        back.start()
+    for back in outs:
+        back.wait()
+
+
+def gated_kernel(k, v, q, packed, q_near):
+    q_near[...] = q[...]
     shape = (packed.shape[0],) + packed.shape[2:]
     packed[:, 0] = (k[...].astype(F32) * v[...].astype(F32)).astype(BF).reshape(shape)
 
@@ -133,6 +145,13 @@
     gr, gi = split(forward(by_channel(got[:, 1]), fwd, tc, ts, mf, mixed))
     lag_spec[...] = join(xr * gr + xi * gi, xr * gi - xi * gr)
     both[:, 1] = by_block(inverse(join(fr * gr + fi * gi, fr * gi - fi * gr), back, tc, ts, mi))
+
+
+def add_kernel(own, other, out, *, scale):
+    total = jnp.swapaxes((own[...] + other[...].astype(F32)) * scale, 0, 1)
+    n = total.shape[-1]
+    for m in range(total.shape[0]):
+        out[:, m * n : (m + 1) * n] = total[m]
 
 
 def out_kernel(both, packed, tokens, k, v, skip, query_out, key_out, value_out):
@@ -162,6 +181,14 @@
 
 def hbm_out(a):
     return pltpu.HBM(a.shape, a.dtype)
+
+
+def vmem(a):
+    return pltpu.with_memory_space_constraint(a, pltpu.VMEM)
+
+
+def vmem_out(a):
+    return pltpu.VMEM(a.shape, a.dtype)
 
 
 def cut(a, dim, grid, at=None):
@@ -214,21 +241,24 @@
         in_specs=[anywhere],
         out_specs=anywhere,
         out_shape=pltpu.HBM((tp, rows.shape[0], chans), BF),
-        scratch_shapes=[pltpu.SemaphoreType.DMA((tp,))],
+        scratch_shapes=[
+            pltpu.VMEM((tp, rows.shape[0], chans), BF),
+            pltpu.SemaphoreType.DMA((2, 2 * tp)),
+        ],
     )(hbm(rows))
     rows = lax.all_to_all(cuts, "tp", split_axis=0, concat_axis=0, tiled=True)
     rows = rows.reshape(block, chans)
 
     grid = 4
     params = pltpu.CompilerParams(vmem_limit_bytes=16 * 2**20)
-    half_packed = pl.pallas_call(
+    half_packed, q_near = pl.pallas_call(
         gated_kernel,
         grid=(grid,),
-        in_specs=[cut(k, 0, grid), cut(v, 0, grid)],
-        out_specs=cut(packed_type, 0, grid, (1, 0)),
-        out_shape=hbm_out(packed_type),
+        in_specs=[cut(k, 0, grid), cut(v, 0, grid), cut(q, 0, grid)],
+        out_specs=[cut(packed_type, 0, grid, (1, 0)), cut(q, 0, grid)],
+        out_shape=[hbm_out(packed_type), vmem_out(q)],
         compiler_params=params,
-    )(hbm(k), hbm(v))
+    )(hbm(k), hbm(v), hbm(q))
     packed = pl.pallas_call(
         grad_kernel,
         grid=(grid,),
@@ -237,8 +267,7 @@
         out_shape=hbm_out(packed_type),
         input_output_aliases={2: 0},
         compiler_params=params,
-    )(rows, hbm(q), hbm(half_packed))
-    (tokens,) = call(tokens_kernel, grid, [(rows, 1)], (), [(hbm_out(chan_type), 0)], 16)
+    )(rows, vmem(q_near), hbm(half_packed))
     got = exchange(packed)
 
     taps = filter_taps[0].reshape(own, ctx, block)
@@ -260,16 +289,21 @@
         ),
         [(struct(half_out, F32), 0), (struct(half_out, BF), 0)], 28,
     )
+    lag_away, rows = lax.optimization_barrier((lag_away, rows))
     other = lax.ppermute(lag_away, "dp", [(j, (j + 1) % dp) for j in range(dp)])
     grad_scale = 1.0 / math.sqrt(dp * ctx * block)
-    filter_out = ((lag_own + other.astype(F32)) * grad_scale).reshape(1, own, -1)
-
+    (filter_out,) = call(
+        functools.partial(add_kernel, scale=grad_scale), 2, [(lag_own, 0), (other, 0)], (),
+        [(hbm_out(struct((own, ctx * block // dp), F32)), 0)], 16,
+    )
+
+    (tokens,) = call(tokens_kernel, grid, [(rows, 1)], (), [(hbm_out(chan_type), 0)], 16)
     query_out, key_out, value_out = call(
         out_kernel, grid,
-        [(both, 0), (packed, 0), (tokens, 0), (hbm(k), 0), (hbm(v), 0), (skip_gain[0].reshape(ctx, own), 0)],
+        [(both, 0), (packed, 0), (hbm(tokens), 0), (hbm(k), 0), (hbm(v), 0), (skip_gain[0].reshape(ctx, own), 0)],
         (), [(hbm_out(chan_type), 0)] * 3, 16,
     )
-    return (query_out[None], key_out[None], value_out[None], filter_out)
+    return (query_out[None], key_out[None], value_out[None], filter_out[None])
 
 
 def solution(mesh):

time: 178 us -> 161 us (0.904)
  Pallas kernels: 40.4 us -> 25.2 us
  waiting for transfers between devices: 97.7 us -> 99.9 us
  local copies, waits for them, and re-layouts: 4.59 us -> 2.65 us
  other arithmetic: 2.54 us -> 0.67 us
    pallas_call x1, Pallas kernels: 17 us -> 1.83 us  [local(): pl.pallas_call(cut_kernel, in_specs=[anywhere], out_specs=anywhere, out_s...]
    all_to_all x2, waiting for transfers between devices: 91.6 us -> 93.9 us  [exchange(): lax.all_to_all(flat, 'ctx', split_axis=0, concat_axis=0, tiled=True)]
    reshape x1 -> x0, local copies, waits for them, and re-layouts: 1.93 us -> none  [local(): ((lag_own + other.astype(F32)) * grad_scale).reshape(1, own, -1)]
    mul x1 -> x0, other arithmetic: 1.87 us -> none  [local(): (lag_own + other.astype(F32)) * grad_scale]
    pallas_call x5 -> x6, Pallas kernels: 16.5 us -> 18.2 us  [call(): pl.pallas_call(body, grid=(grid,), in_specs=[cut(a, d, grid) for a, d in...]
  transfers between devices with their start and end apart: 4 -> 4, of which waited for: 3 -> 3; matrix products, arithmetic and copies ran while one was open for 3% -> 1% of each run, Pallas kernels for 5% -> 7%
where the time goes in v4:
time: 161 us; the launch traced here: 160 us
  waiting for transfers between devices  99.9 us (62%)
  starting transfers between devices  31.2 us (19%)
  Pallas kernels  25.2 us (16%)
  local copies, waits for them, and re-layouts  2.65 us (2%)
    all_to_all x2, waiting for transfers between devices, exchange(): lax.all_to_all(flat, 'ctx', split_axis=0, concat_axis=0, tiled=True)  93.9 us
    all_to_all x2, starting transfers between devices, exchange(): lax.all_to_all(flat, 'ctx', split_axis=0, concat_axis=0, tiled=True)  25 us
    pallas_call x6, Pallas kernels, call(): pl.pallas_call(body, grid=(grid,), in_specs=[cut(a, d, grid) for a, d in...  18.2 us
    all_to_all x1, waiting for transfers between devices, local(): rows = lax.all_to_all(cuts, 'tp', split_axis=0, concat_axis=0, tiled=True)  5.99 us
    all_to_all x1, starting transfers between devices, local(): rows = lax.all_to_all(cuts, 'tp', split_axis=0, concat_axis=0, tiled=True)  4.3 us
    pallas_call x1, Pallas kernels, local(): pl.pallas_call(gated_kernel, grid=(grid,), in_specs=[cut(k, 0, grid), cut...  3.48 us
  transfers between devices with their start and end apart: 4, of which 3 were waited for; matrix products, arithmetic and copies ran while one was open for 1% of the time, Pallas kernels for 7%

profile of v4, /device:TPU:8, one launch (start us, length us, event | category | flops | bytes accessed | tf_op | source)
XLA Modules:
  0.0 160.4 jit_solution(3317809223081310992)
XLA Ops:
  0.6 1.8 %shard_map.147 = bf16[4,32,2048]{2,1,0:T(8,128)(2,1)} custom-call(bf16[32,8192]{1,0:T(8,128)(2,1)} %bitcast.31), custom_call_target="tpu_custom_call" | custom-call | tf_op jit(solution)/shard_map/pallas_call | solution.py:239
  2.5 4.3 %all-to-all-start = ((bf16[4,32,2048]{2,1,0:T(8,128)(2,1)}), bf16[4,32,2048]{2,1,0:T(8,128)(2,1)S(1)}, u32[]{:S(2)}, u32[]{:S(2)}) async-start(bf16[4,32,2048]{2,1,0:T(8,128)(2,1)} %shard_map.147), calls=%async_computation | async-start | bytes 1048576 | tf_op jit(solution)/shard_map/all_to_all | solution.py:249
  6.8 3.5 %shard_map.148 = (bf16[64,2,32,128]{3,2,1,0:T(8,128)(2,1)}, bf16[2048,128]{1,0:T(8,128)(2,1)S(1)}) custom-call(bf16[2048,128]{1,0:T(8,128)(2,1)} %bitcast.25, bf16[2048,128]{1,0:T(8,128)(2,1)} %bitcast.27, bf16[2048,128]{1,0:T(8,128)(2,1)} %bitcast.30), custom_call_target="tpu_custom_call" | custom-call | tf_op jit(solution)/shard_map/pallas_call | solution.py:254
  10.3 6.0 %all-to-all-done = bf16[4,32,2048]{2,1,0:T(8,128)(2,1)S(1)} async-done(((bf16[4,32,2048]{2,1,0:T(8,128)(2,1)}), bf16[4,32,2048]{2,1,0:T(8,128)(2,1)S(1)}, u32[]{:S(2)}, u32[]{:S(2)}) %all-to-all-start) | async-done | bytes 524320 | tf_op jit(solution)/shard_map/all_to_all | solution.py:249
  16.3 0.0 copy-start.2
  16.3 1.7 %shard_map.149.packed = bf16[64,2,32,128]{3,2,1,0:T(8,128)(2,1)} custom-call(bf16[128,2048]{1,0:T(8,128)(2,1)S(1)} %bitcast.21, bf16[2048,128]{1,0:T(8,128)(2,1)S(1)} %get-tuple-element.15.q, bf16[64,2,32,128]{3,2,1,0:T(8,128)(2,1)} %get-tuple-element.16.half_packed), custom_call_target="tpu_custom_call", output_to_operand_aliasing={{}: (2, {})} | custom-call | tf_op jit(solution)/shard_map/pallas_call | solution.py:262
  18.0 18.9 %all-to-all-start.1 = ((bf16[64,64,128]{2,1,0:T(8,128)(2,1)}), bf16[64,64,128]{2,1,0:T(8,128)(2,1)}, u32[]{:S(2)}, u32[]{:S(2)}) async-start(bf16[64,64,128]{2,1,0:T(8,128)(2,1)} %bitcast.20), calls=%async_computation.1 | async-start | bytes 2097152 | tf_op jit(solution)/shard_map/all_to_all | solution.py:235
  36.9 0.0 copy-done.2
  36.9 0.1 copy.17
  37.0 2.2 %shard_map.150.f_spec = f32[2560,256]{1,0:T(8,128)S(1)} custom-call(bf16[32,64,128]{2,1,0:T(8,128)(2,1)S(1)} %bitcast.24, bf16[160,64]{1,0:T(8,128)(2,1)} %constant.31.clone.fwd, f32[80,256]{1,0:T(8,128)} %constant.33.clone.tc, f32[80,256]{1,0:T(8,128)} %constant.34.clone.ts, bf16[256,256]{1,0:T(8,128)(2,1)} %constant.35.clone.mf), custom_call_target="tpu_custom_call" | custom-call | flops 1048576 | bytes 1048576 | tf_op jit(solution)/shard_map/pallas_call | solution.py:205
  39.3 51.2 %all-to-all-done.1 = bf16[64,64,128]{2,1,0:T(8,128)(2,1)} async-done(((bf16[64,64,128]{2,1,0:T(8,128)(2,1)}), bf16[64,64,128]{2,1,0:T(8,128)(2,1)}, u32[]{:S(2)}, u32[]{:S(2)}) %all-to-all-start.1) | async-done | bytes 1048608 | tf_op jit(solution)/shard_map/all_to_all | solution.py:235
  90.5 0.0 copy-start.3
  90.5 6.5 %shard_map.151 = (bf16[64,2,32,128]{3,2,1,0:T(8,128)(2,1)}, bf16[2560,256]{1,0:T(8,128)(2,1)}) custom-call(bf16[64,2,32,128]{3,2,1,0:T(8,128)(2,1)} %bitcast.6.got, f32[2560,256]{1,0:T(8,128)S(1)} %shard_map.150.f_spec, bf16[160,64]{1,0:T(8,128)(2,1)} %constant.31.clone.fwd, bf16[64,160]{1,0:T(8,128)(2,1)} %constant.32.clone.back, ...), custom_call_target="tpu_custom_call" | custom-call | flops 1048576 | bytes 1048576 | tf_op jit(solution)/shard_map/pallas_call | solution.py:205
  97.0 0.0 copy-start.4
  97.0 0.0 copy-start
  97.0 6.1 %all-to-all-start.2 = ((bf16[64,64,128]{2,1,0:T(8,128)(2,1)}), bf16[64,64,128]{2,1,0:T(8,128)(2,1)S(1)}, u32[]{:S(2)}, u32[]{:S(2)}) async-start(bf16[64,64,128]{2,1,0:T(8,128)(2,1)} %bitcast.29), calls=%async_computation.2 | async-start | bytes 2097152 | tf_op jit(solution)/shard_map/all_to_all | solution.py:235
  103.1 0.0 copy-done.3
  103.1 0.6 dynamic-slice_bitcast_fusion
  103.7 0.0 copy-start.1
  103.7 1.3 copy-done.1
  105.1 2.9 %shard_map.152 = (f32[32,32,128]{2,1,0:T(8,128)S(1)}, bf16[32,32,128]{2,1,0:T(8,128)(2,1)}) custom-call(bf16[2560,256]{1,0:T(8,128)(2,1)S(1)} %copy-done.1, bf16[32,160]{1,0:T(8,128)(2,1)} %get-tuple-element.27.own_rows, bf16[32,160]{1,0:T(8,128)(2,1)} %get-tuple-element.26.away_rows, f32[80,256]{1,0:T(8,128)} %constant.33.clone.tc, ...), custom_call_target="tpu_custom_call" | custom-call | flops 1048576 | bytes 1048576 | tf_op jit(solution)/shard_map/pallas_call | solution.py:205
  108.0 1.9 %collective-permute-start = (bf16[32,32,128]{2,1,0:T(8,128)(2,1)}, bf16[32,32,128]{2,1,0:T(8,128)(2,1)S(1)}, u32[]{:S(2)}, u32[]{:S(2)}) collective-permute-start(bf16[32,32,128]{2,1,0:T(8,128)(2,1)} %get-tuple-element.25), channel_id=1, source_target_pairs={{0,256},{256,0},{1,257},{257,1},{2,258},{258,2},{3,259},{259,3},{4... | collective-permute-start | bytes 786440 | tf_op jit(solution)/shard_map/ppermute | solution.py:293
  109.9 0.5 broadcast.4
  110.4 0.0 copy-done.4
  110.4 0.7 reduce.3
  111.1 0.1 reshape_squeeze.7.skip
  111.2 1.7 %shard_map.153.tokens = bf16[2048,128]{1,0:T(8,128)(2,1)} custom-call(bf16[128,2048]{1,0:T(8,128)(2,1)S(1)} %bitcast.22), custom_call_target="tpu_custom_call" | custom-call | flops 1048576 | bytes 1048576 | tf_op jit(solution)/shard_map/pallas_call | solution.py:205
  112.9 0.0 collective-permute-done.other
  112.9 0.9 shard_map.155
  113.7 42.7 %all-to-all-done.2 = bf16[64,64,128]{2,1,0:T(8,128)(2,1)S(1)} async-done(((bf16[64,64,128]{2,1,0:T(8,128)(2,1)}), bf16[64,64,128]{2,1,0:T(8,128)(2,1)S(1)}, u32[]{:S(2)}, u32[]{:S(2)}) %all-to-all-start.2) | async-done | bytes 1048608 | tf_op jit(solution)/shard_map/all_to_all | solution.py:235
  156.4 0.0 copy-done
  156.4 4.0 %shard_map.154 = (bf16[2048,128]{1,0:T(8,128)(2,1)}, bf16[2048,128]{1,0:T(8,128)(2,1)}, bf16[2048,128]{1,0:T(8,128)(2,1)}) custom-call(bf16[64,2,32,128]{3,2,1,0:T(8,128)(2,1)S(1)} %bitcast.23, bf16[64,2,32,128]{3,2,1,0:T(8,128)(2,1)S(1)} %copy-done, bf16[2048,128]{1,0:T(8,128)(2,1)} %shard_map.153.tokens, bf16[2048,128]{1,0:T(8,128)(2,1)} %bitcast.26, ...), custom_call_target="tpu_custom_call" | custom-call | flops 1048576 | bytes 1048576 | tf_op jit(solution)/shard_map/pallas_call | solution.py:205
Async XLA Ops:
  2.5 13.8 %all-to-all-start = ((bf16[4,32,2048]{2,1,0:T(8,128)(2,1)}), bf16[4,32,2048]{2,1,0:T(8,128)(2,1)S(1)}, u32[]{:S(2)}, u32[]{:S(2)}) async-start(bf16[4,32,2048]{2,1,0:T(8,128)(2,1)} %shard_map.147), calls=%async_computation | async-start | bytes 1048576 | tf_op jit(solution)/shard_map/all_to_all | solution.py:249
  16.3 20.7 %copy-start.2 = (bf16[1,32,8192]{2,1,0:T(8,128)(2,1)S(1)}, bf16[1,32,8192]{2,1,0:T(8,128)(2,1)}, u32[]{:S(2)}) copy-start(bf16[1,32,8192]{2,1,0:T(8,128)(2,1)} %param.16) | copy-start | bytes 1572868
  18.0 72.5 %all-to-all-start.1 = ((bf16[64,64,128]{2,1,0:T(8,128)(2,1)}), bf16[64,64,128]{2,1,0:T(8,128)(2,1)}, u32[]{:S(2)}, u32[]{:S(2)}) async-start(bf16[64,64,128]{2,1,0:T(8,128)(2,1)} %bitcast.20), calls=%async_computation.1 | async-start | bytes 2097152 | tf_op jit(solution)/shard_map/all_to_all | solution.py:235
  90.5 12.6 %copy-start.3 = (bf16[2,32,160]{2,1,0:T(8,128)(2,1)S(1)}, bf16[2,32,160]{2,1,0:T(8,128)(2,1)}, u32[]{:S(2)}) copy-start(bf16[2,32,160]{2,1,0:T(8,128)(2,1)} %constant.43) | copy-start | bytes 61444
  97.0 13.4 %copy-start.4 = (f32[1,2048]{1,0:T(1,128)S(1)}, f32[1,2048]{1,0:T(1,128)}, u32[]{:S(2)}) copy-start(f32[1,2048]{1,0:T(1,128)} %param.17) | copy-start | bytes 24580
  97.0 59.4 %copy-start = (bf16[64,2,32,128]{3,2,1,0:T(8,128)(2,1)S(1)}, bf16[64,2,32,128]{3,2,1,0:T(8,128)(2,1)}, u32[]{:S(2)}) copy-start(bf16[64,2,32,128]{3,2,1,0:T(8,128)(2,1)} %shard_map.149.packed) | copy-start | bytes 3145732
  97.0 59.4 %all-to-all-start.2 = ((bf16[64,64,128]{2,1,0:T(8,128)(2,1)}), bf16[64,64,128]{2,1,0:T(8,128)(2,1)S(1)}, u32[]{:S(2)}, u32[]{:S(2)}) async-start(bf16[64,64,128]{2,1,0:T(8,128)(2,1)} %bitcast.29), calls=%async_computation.2 | async-start | bytes 2097152 | tf_op jit(solution)/shard_map/all_to_all | solution.py:235
  103.7 1.3 copy-start.1
  108.0 4.9 %collective-permute-start = (bf16[32,32,128]{2,1,0:T(8,128)(2,1)}, bf16[32,32,128]{2,1,0:T(8,128)(2,1)S(1)}, u32[]{:S(2)}, u32[]{:S(2)}) collective-permute-start(bf16[32,32,128]{2,1,0:T(8,128)(2,1)} %get-tuple-element.25), channel_id=1, source_target_pairs={{0,256},{256,0},{1,257},{257,1},{2,258},{258,2},{3,259},{259,3},{4... | collective-permute-start | bytes 786440 | tf_op jit(solution)/shard_map/ppermute | solution.py:293

commit v5 on v4

--- a/solution.py
+++ b/solution.py
@@ -130,8 +130,10 @@
     packed[:, 0] = (rows[...].astype(F32).T * q[...].astype(F32)).astype(BF).reshape(shape)
 
 
-def tokens_kernel(rows, tokens):
-    tokens[...] = rows[...].astype(F32).T.astype(BF)
+def near_kernel(rows, k, v, near):
+    near[0] = rows[...].astype(F32).T.astype(BF)
+    near[1] = k[...]
+    near[2] = v[...]
 
 
 def filter_kernel(taps, fwd, tc, ts, mf, f_spec, mixed):
@@ -154,16 +156,17 @@
         out[:, m * n : (m + 1) * n] = total[m]
 
 
-def out_kernel(both, packed, tokens, k, v, skip, query_out, key_out, value_out):
-    shape = tokens.shape
+def out_kernel(both, packed, near, skip, query_out, key_out, value_out):
+    shape = query_out.shape
+    tokens, k, v = (near[i].astype(F32) for i in range(3))
     s = lax.broadcast_in_dim(skip[...], skip.shape + (shape[1],), (0, 1))
     conv, corr = (both[:, i].astype(F32) for i in range(2))
     gated, grad = (packed[:, i].astype(F32) for i in range(2))
     through = (conv + s * gated).reshape(shape)
-    query_out[...] = (tokens[...].astype(F32) * through).astype(BF)
+    query_out[...] = (tokens * through).astype(BF)
     total = (corr + s * grad).reshape(shape)
-    key_out[...] = (total * v[...].astype(F32)).astype(BF)
-    value_out[...] = (total * k[...].astype(F32)).astype(BF)
+    key_out[...] = (total * v).astype(BF)
+    value_out[...] = (total * k).astype(BF)
 
 
 def lag_kernel(lag_spec, own_rows, away_rows, tc, ts, mi, own, away):
@@ -249,7 +252,7 @@
     rows = lax.all_to_all(cuts, "tp", split_axis=0, concat_axis=0, tiled=True)
     rows = rows.reshape(block, chans)
 
-    grid = 4
+    grid = 2
     params = pltpu.CompilerParams(vmem_limit_bytes=16 * 2**20)
     half_packed, q_near = pl.pallas_call(
         gated_kernel,
@@ -289,7 +292,6 @@
         ),
         [(struct(half_out, F32), 0), (struct(half_out, BF), 0)], 28,
     )
-    lag_away, rows = lax.optimization_barrier((lag_away, rows))
     other = lax.ppermute(lag_away, "dp", [(j, (j + 1) % dp) for j in range(dp)])
     grad_scale = 1.0 / math.sqrt(dp * ctx * block)
     (filter_out,) = call(
@@ -297,10 +299,14 @@
         [(hbm_out(struct((own, ctx * block // dp), F32)), 0)], 16,
     )
 
-    (tokens,) = call(tokens_kernel, grid, [(rows, 1)], (), [(hbm_out(chan_type), 0)], 16)
+    filter_out, rows = lax.optimization_barrier((filter_out, rows))
+    (near,) = call(
+        near_kernel, grid, [(rows, 1), (hbm(k), 0), (hbm(v), 0)], (),
+        [(vmem_out(struct((3, chans, block), BF)), 1)], 16,
+    )
     query_out, key_out, value_out = call(
         out_kernel, grid,
-        [(both, 0), (packed, 0), (hbm(tokens), 0), (hbm(k), 0), (hbm(v), 0), (skip_gain[0].reshape(ctx, own), 0)],
+        [(both, 0), (packed, 0), (vmem(near), 1), (skip_gain[0].reshape(ctx, own), 0)],
         (), [(hbm_out(chan_type), 0)] * 3, 16,
     )
     return (query_out[None], key_out[None], value_out[None], filter_out[None])

time: 161 us -> 159 us (0.988)
  Pallas kernels: 25.2 us -> 21 us
  waiting for transfers between devices: 99.9 us -> 103 us
    pallas_call x6, Pallas kernels: 18.2 us -> 16 us  [call(): pl.pallas_call(body, grid=(grid,), in_specs=[cut(a, d, grid) for a, d in...]
    all_to_all x2, waiting for transfers between devices: 93.9 us -> 95.6 us  [exchange(): lax.all_to_all(flat, 'ctx', split_axis=0, concat_axis=0, tiled=True)]
  transfers between devices with their start and end apart: 4 -> 4, of which waited for: 3 -> 4; matrix products, arithmetic and copies ran while one was open for 1% -> 1% of each run, Pallas kernels for 7% -> 6%
where the time goes in v5:
time: 159 us
  waiting for transfers between devices  103 us (65%)
  starting transfers between devices  31.6 us (20%)
  Pallas kernels  21 us (13%)
    all_to_all x2, waiting for transfers between devices, exchange(): lax.all_to_all(flat, 'ctx', split_axis=0, concat_axis=0, tiled=True)  95.6 us
    all_to_all x2, starting transfers between devices, exchange(): lax.all_to_all(flat, 'ctx', split_axis=0, concat_axis=0, tiled=True)  25.3 us
    pallas_call x6, Pallas kernels, call(): pl.pallas_call(body, grid=(grid,), in_specs=[cut(a, d, grid) for a, d in...  16 us
    all_to_all x1, waiting for transfers between devices, local(): rows = lax.all_to_all(cuts, 'tp', split_axis=0, concat_axis=0, tiled=True)  7.35 us
    all_to_all x1, starting transfers between devices, local(): rows = lax.all_to_all(cuts, 'tp', split_axis=0, concat_axis=0, tiled=True)  4.3 us
  transfers between devices with their start and end apart: 4, of which 4 were waited for; matrix products, arithmetic and copies ran while one was open for 1% of the time, Pallas kernels for 6%

profile of v5, /device:TPU:8, one launch (start us, length us, event | category | flops | bytes accessed | tf_op | source)
XLA Modules:
  0.0 158.5 jit_solution(12834785514479618941)
XLA Ops:
  0.6 1.8 %shard_map.147 = bf16[4,32,2048]{2,1,0:T(8,128)(2,1)} custom-call(bf16[32,8192]{1,0:T(8,128)(2,1)} %bitcast.30), custom_call_target="tpu_custom_call" | custom-call | tf_op jit(solution)/shard_map/pallas_call | solution.py:242
  2.5 4.3 %all-to-all-start = ((bf16[4,32,2048]{2,1,0:T(8,128)(2,1)}), bf16[4,32,2048]{2,1,0:T(8,128)(2,1)S(1)}, u32[]{:S(2)}, u32[]{:S(2)}) async-start(bf16[4,32,2048]{2,1,0:T(8,128)(2,1)} %shard_map.147), calls=%async_computation | async-start | bytes 1048576 | tf_op jit(solution)/shard_map/all_to_all | solution.py:252
  6.8 2.1 %shard_map.148 = (bf16[64,2,32,128]{3,2,1,0:T(8,128)(2,1)}, bf16[2048,128]{1,0:T(8,128)(2,1)S(1)}) custom-call(bf16[2048,128]{1,0:T(8,128)(2,1)} %bitcast.24, bf16[2048,128]{1,0:T(8,128)(2,1)} %bitcast.26, bf16[2048,128]{1,0:T(8,128)(2,1)} %bitcast.29), custom_call_target="tpu_custom_call" | custom-call | tf_op jit(solution)/shard_map/pallas_call | solution.py:257
  8.9 7.3 %all-to-all-done = bf16[4,32,2048]{2,1,0:T(8,128)(2,1)S(1)} async-done(((bf16[4,32,2048]{2,1,0:T(8,128)(2,1)}), bf16[4,32,2048]{2,1,0:T(8,128)(2,1)S(1)}, u32[]{:S(2)}, u32[]{:S(2)}) %all-to-all-start) | async-done | bytes 524320 | tf_op jit(solution)/shard_map/all_to_all | solution.py:252
  16.3 1.1 shard_map.149.packed
  17.3 0.0 copy-start.2
  17.3 19.0 %all-to-all-start.1 = ((bf16[64,64,128]{2,1,0:T(8,128)(2,1)}), bf16[64,64,128]{2,1,0:T(8,128)(2,1)}, u32[]{:S(2)}, u32[]{:S(2)}) async-start(bf16[64,64,128]{2,1,0:T(8,128)(2,1)} %bitcast.20), calls=%async_computation.1 | async-start | bytes 2097152 | tf_op jit(solution)/shard_map/all_to_all | solution.py:238
  36.4 0.0 copy-done.2
  36.4 0.1 copy.17
  36.5 2.2 %shard_map.150.f_spec = f32[2560,256]{1,0:T(8,128)S(1)} custom-call(bf16[32,64,128]{2,1,0:T(8,128)(2,1)S(1)} %bitcast.23, bf16[160,64]{1,0:T(8,128)(2,1)} %constant.31.clone.fwd, f32[80,256]{1,0:T(8,128)} %constant.33.clone.tc, f32[80,256]{1,0:T(8,128)} %constant.34.clone.ts, bf16[256,256]{1,0:T(8,128)(2,1)} %constant.35.clone.mf), custom_call_target="tpu_custom_call" | custom-call | flops 1048576 | bytes 1048576 | tf_op jit(solution)/shard_map/pallas_call | solution.py:208
  38.8 51.2 %all-to-all-done.1 = bf16[64,64,128]{2,1,0:T(8,128)(2,1)} async-done(((bf16[64,64,128]{2,1,0:T(8,128)(2,1)}), bf16[64,64,128]{2,1,0:T(8,128)(2,1)}, u32[]{:S(2)}, u32[]{:S(2)}) %all-to-all-start.1) | async-done | bytes 1048608 | tf_op jit(solution)/shard_map/all_to_all | solution.py:238
  90.0 6.4 %shard_map.151 = (bf16[64,2,32,128]{3,2,1,0:T(8,128)(2,1)}, bf16[2560,256]{1,0:T(8,128)(2,1)}) custom-call(bf16[64,2,32,128]{3,2,1,0:T(8,128)(2,1)} %bitcast.6.got, f32[2560,256]{1,0:T(8,128)S(1)} %shard_map.150.f_spec, bf16[160,64]{1,0:T(8,128)(2,1)} %constant.31.clone.fwd, bf16[64,160]{1,0:T(8,128)(2,1)} %constant.32.clone.back, ...), custom_call_target="tpu_custom_call" | custom-call | flops 1048576 | bytes 1048576 | tf_op jit(solution)/shard_map/pallas_call | solution.py:208
  96.4 0.0 copy-start.3
  96.4 0.0 copy-start.1
  96.4 0.0 copy-start.4
  96.4 6.3 %all-to-all-start.2 = ((bf16[64,64,128]{2,1,0:T(8,128)(2,1)}), bf16[64,64,128]{2,1,0:T(8,128)(2,1)}, u32[]{:S(2)}, u32[]{:S(2)}) async-start(bf16[64,64,128]{2,1,0:T(8,128)(2,1)} %bitcast.28), calls=%async_computation.2 | async-start | bytes 2097152 | tf_op jit(solution)/shard_map/all_to_all | solution.py:238
  102.7 0.0 copy-done.3
  102.7 0.6 dynamic-slice_bitcast_fusion
  103.3 0.0 copy-done.1
  103.3 2.3 %shard_map.152 = (f32[32,32,128]{2,1,0:T(8,128)S(1)}, bf16[32,32,128]{2,1,0:T(8,128)(2,1)S(1)}) custom-call(bf16[2560,256]{1,0:T(8,128)(2,1)S(1)} %copy-done.1, bf16[32,160]{1,0:T(8,128)(2,1)} %get-tuple-element.27.own_rows, bf16[32,160]{1,0:T(8,128)(2,1)} %get-tuple-element.26.away_rows, f32[80,256]{1,0:T(8,128)} %constant.33.clone.tc, ...), custom_call_target="tpu_custom_call" | custom-call | flops 1048576 | bytes 1048576 | tf_op jit(solution)/shard_map/pallas_call | solution.py:208
  105.6 1.9 %collective-permute-start = (bf16[32,32,128]{2,1,0:T(8,128)(2,1)S(1)}, bf16[32,32,128]{2,1,0:T(8,128)(2,1)S(1)}, u32[]{:S(2)}, u32[]{:S(2)}) collective-permute-start(bf16[32,32,128]{2,1,0:T(8,128)(2,1)S(1)} %get-tuple-element.20), channel_id=1, source_target_pairs={{0,256},{256,0},{1,257},{257,1},{2,258},{258,2},{3,259},{259,3},{4... | collective-permute-start | bytes 786440 | tf_op jit(solution)/shard_map/ppermute | solution.py:295
  107.5 0.5 broadcast.4
  108.0 0.0 copy-done.4
  108.0 0.7 reduce.3
  108.7 0.1 reshape_squeeze.7.skip
  108.8 0.2 collective-permute-done.other
  109.0 0.9 shard_map.153
  109.9 0.0 copy-start
  109.9 1.6 %shard_map.154.near = bf16[3,2048,128]{2,1,0:T(8,128)(2,1)S(1)} custom-call(bf16[128,2048]{1,0:T(8,128)(2,1)S(1)} %bitcast.22, bf16[2048,128]{1,0:T(8,128)(2,1)} %bitcast.25, bf16[2048,128]{1,0:T(8,128)(2,1)} %bitcast.27), custom_call_target="tpu_custom_call" | custom-call | flops 1048576 | bytes 1048576 | tf_op jit(solution)/shard_map/pallas_call | solution.py:208
  111.5 44.4 %all-to-all-done.2 = bf16[64,64,128]{2,1,0:T(8,128)(2,1)} async-done(((bf16[64,64,128]{2,1,0:T(8,128)(2,1)}), bf16[64,64,128]{2,1,0:T(8,128)(2,1)}, u32[]{:S(2)}, u32[]{:S(2)}) %all-to-all-start.2) | async-done | bytes 1048608 | tf_op jit(solution)/shard_map/all_to_all | solution.py:238
  155.9 0.0 copy-done
  155.9 2.6 %shard_map.155 = (bf16[2048,128]{1,0:T(8,128)(2,1)}, bf16[2048,128]{1,0:T(8,128)(2,1)}, bf16[2048,128]{1,0:T(8,128)(2,1)}) custom-call(bf16[64,2,32,128]{3,2,1,0:T(8,128)(2,1)} %bitcast.8.both, bf16[64,2,32,128]{3,2,1,0:T(8,128)(2,1)S(1)} %copy-done, bf16[3,2048,128]{2,1,0:T(8,128)(2,1)S(1)} %shard_map.154.near, f32[64,32]{1,0:T(8,128)S(1)} %reshape_squeeze.7.skip), custom_call_target="tpu_custom_call" | custom-call | flops 1048576 | bytes 1048576 | tf_op jit(solution)/shard_map/pallas_call | solution.py:208
Async XLA Ops:
  2.5 13.8 %all-to-all-start = ((bf16[4,32,2048]{2,1,0:T(8,128)(2,1)}), bf16[4,32,2048]{2,1,0:T(8,128)(2,1)S(1)}, u32[]{:S(2)}, u32[]{:S(2)}) async-start(bf16[4,32,2048]{2,1,0:T(8,128)(2,1)} %shard_map.147), calls=%async_computation | async-start | bytes 1048576 | tf_op jit(solution)/shard_map/all_to_all | solution.py:252
  17.3 19.1 %copy-start.2 = (bf16[1,32,8192]{2,1,0:T(8,128)(2,1)S(1)}, bf16[1,32,8192]{2,1,0:T(8,128)(2,1)}, u32[]{:S(2)}) copy-start(bf16[1,32,8192]{2,1,0:T(8,128)(2,1)} %param.16) | copy-start | bytes 1572868
  17.3 72.7 %all-to-all-start.1 = ((bf16[64,64,128]{2,1,0:T(8,128)(2,1)}), bf16[64,64,128]{2,1,0:T(8,128)(2,1)}, u32[]{:S(2)}, u32[]{:S(2)}) async-start(bf16[64,64,128]{2,1,0:T(8,128)(2,1)} %bitcast.20), calls=%async_computation.1 | async-start | bytes 2097152 | tf_op jit(solution)/shard_map/all_to_all | solution.py:238
  96.4 6.3 %copy-start.3 = (bf16[2,32,160]{2,1,0:T(8,128)(2,1)S(1)}, bf16[2,32,160]{2,1,0:T(8,128)(2,1)}, u32[]{:S(2)}) copy-start(bf16[2,32,160]{2,1,0:T(8,128)(2,1)} %constant.43) | copy-start | bytes 61444
  96.4 7.0 %copy-start.1 = (bf16[2560,256]{1,0:T(8,128)(2,1)S(1)}, bf16[2560,256]{1,0:T(8,128)(2,1)}, u32[]{:S(2)}) copy-start(bf16[2560,256]{1,0:T(8,128)(2,1)} %get-tuple-element.18.lag_spec) | copy-start | bytes 3932164
  96.4 11.7 %copy-start.4 = (f32[1,2048]{1,0:T(1,128)S(1)}, f32[1,2048]{1,0:T(1,128)}, u32[]{:S(2)}) copy-start(f32[1,2048]{1,0:T(1,128)} %param.17) | copy-start | bytes 24580
  96.4 59.5 %all-to-all-start.2 = ((bf16[64,64,128]{2,1,0:T(8,128)(2,1)}), bf16[64,64,128]{2,1,0:T(8,128)(2,1)}, u32[]{:S(2)}, u32[]{:S(2)}) async-start(bf16[64,64,128]{2,1,0:T(8,128)(2,1)} %bitcast.28), calls=%async_computation.2 | async-start | bytes 2097152 | tf_op jit(solution)/shard_map/all_to_all | solution.py:238
  105.6 3.4 %collective-permute-start = (bf16[32,32,128]{2,1,0:T(8,128)(2,1)S(1)}, bf16[32,32,128]{2,1,0:T(8,128)(2,1)S(1)}, u32[]{:S(2)}, u32[]{:S(2)}) collective-permute-start(bf16[32,32,128]{2,1,0:T(8,128)(2,1)S(1)} %get-tuple-element.20), channel_id=1, source_target_pairs={{0,256},{256,0},{1,257},{257,1},{2,258},{258,2},{3,259},{259,3},{4... | collective-permute-start | bytes 786440 | tf_op jit(solution)/shard_map/ppermute | solution.py:295
  109.9 46.0 %copy-start = (bf16[64,2,32,128]{3,2,1,0:T(8,128)(2,1)S(1)}, bf16[64,2,32,128]{3,2,1,0:T(8,128)(2,1)}, u32[]{:S(2)}) copy-start(bf16[64,2,32,128]{3,2,1,0:T(8,128)(2,1)} %shard_map.149.packed) | copy-start | bytes 3145732

commit v6 on v5

--- a/solution.py
+++ b/solution.py
@@ -140,13 +140,54 @@
     f_spec[...] = forward([taps[c] for c in range(taps.shape[0])], fwd, tc, ts, mf, mixed)
 
 
-def main_kernel(got, f_spec, fwd, back, tc, ts, mf, mi, both, lag_spec, mixed):
-    fr, fi = split(f_spec[...])
-    xr, xi = split(forward(by_channel(got[:, 0]), fwd, tc, ts, mf, mixed))
-    both[:, 0] = by_block(inverse(join(fr * xr - fi * xi, fr * xi + fi * xr), back, tc, ts, mi))
-    gr, gi = split(forward(by_channel(got[:, 1]), fwd, tc, ts, mf, mixed))
-    lag_spec[...] = join(xr * gr + xi * gi, xr * gi - xi * gr)
-    both[:, 1] = by_block(inverse(join(fr * gr + fi * gi, fr * gi - fi * gr), back, tc, ts, mi))
+def main_kernel(got, f_spec, *refs):
+    tables, both, lag_spec = refs[:6], refs[6], refs[7]
+    near, got_v, f_v, both_v, lag_v, mixed, table_sems, sems = (
+        refs[8:14], *refs[14:21]
+    )
+    half = got_v.shape[3]
+    rows = f_v.shape[1]
+    copy = pltpu.make_async_copy
+
+    def piece(ref, h, p):
+        return ref.at[:, p, pl.ds(h * half, half)]
+
+    def span(ref, h):
+        return ref.at[pl.ds(h * rows, rows)]
+
+    table_in = [copy(t, n, table_sems.at[i]) for i, (t, n) in enumerate(zip(tables, near))]
+    got_in = [[copy(piece(got, h, p), got_v.at[h, p], sems.at[0, h, p]) for p in (0, 1)] for h in (0, 1)]
+    f_in = [copy(span(f_spec, h), f_v.at[h], sems.at[1, h, 0]) for h in (0, 1)]
+    out = [[copy(both_v.at[h, p], piece(both, h, p), sems.at[2, h, p]) for p in (0, 1)] for h in (0, 1)]
+    lag_out = [copy(lag_v.at[h], span(lag_spec, h), sems.at[1, h, 1]) for h in (0, 1)]
+    got_in[0][0].start()
+    for t in table_in:
+        t.start()
+    f_in[0].start()
+    got_in[0][1].start()
+    got_in[1][0].start()
+    f_in[1].start()
+    got_in[1][1].start()
+    for t in table_in:
+        t.wait()
+    fwd, back, tc, ts, mf, mi = near
+    for h in (0, 1):
+        got_in[h][0].wait()
+        xr, xi = split(forward(by_channel(got_v[h, 0]), fwd, tc, ts, mf, mixed))
+        f_in[h].wait()
+        fr, fi = split(f_v[h])
+        both_v[h, 0] = by_block(inverse(join(fr * xr - fi * xi, fr * xi + fi * xr), back, tc, ts, mi))
+        out[h][0].start()
+        got_in[h][1].wait()
+        gr, gi = split(forward(by_channel(got_v[h, 1]), fwd, tc, ts, mf, mixed))
+        lag_v[h] = join(xr * gr + xi * gi, xr * gi - xi * gr)
+        lag_out[h].start()
+        both_v[h, 1] = by_block(inverse(join(fr * gr + fi * gi, fr * gi - fi * gr), back, tc, ts, mi))
+        out[h][1].start()
+    for h in (0, 1):
+        lag_out[h].wait()
+        for p in (0, 1):
+            out[h][p].wait()
 
 
 def add_kernel(own, other, out, *, scale):
@@ -275,10 +316,25 @@
 
     taps = filter_taps[0].reshape(own, ctx, block)
     (f_spec,) = call(filter_kernel, 2, [(taps, 0)], (fwd, tc, ts, mf), [(spec, 0)], 20, mixed)
-    both, lag_spec = call(
-        main_kernel, 2, [(got, 2), (f_spec, 0)], (fwd, back, tc, ts, mf, mi),
-        [(hbm_out(packed_type), 2), (hbm_out(struct(spec.shape, BF)), 0)], 32, mixed,
-    )
+    tables = (fwd, back, tc, ts, mf, mi)
+    both, lag_spec = pl.pallas_call(
+        main_kernel,
+        in_specs=[anywhere] * 8,
+        out_specs=[anywhere] * 2,
+        out_shape=[hbm_out(packed_type), pltpu.HBM(spec.shape, BF)],
+        scratch_shapes=[pltpu.VMEM(t.shape, t.dtype) for t in tables]
+        + [
+            pltpu.VMEM((2, 2, ctx, own // 2, block), BF),
+            pltpu.VMEM((2, spec.shape[0] // 2, spec.shape[1]), F32),
+            pltpu.VMEM((2, 2, ctx, own // 2, block), BF),
+            pltpu.VMEM((2, spec.shape[0] // 2, spec.shape[1]), BF),
+            pltpu.VMEM(mixed, BF),
+            pltpu.SemaphoreType.DMA((len(tables),)),
+            pltpu.SemaphoreType.DMA((3, 2, 2)),
+        ],
+        compiler_params=pltpu.CompilerParams(vmem_limit_bytes=32 * 2**20),
+        cost_estimate=pl.CostEstimate(flops=2**20, bytes_accessed=2**20, transcendentals=0),
+    )(got, f_spec, *[hbm(t) for t in tables])
     both = exchange(both)
 
     halves = back.reshape(dp, ctx // dp, -1)

time: 159 us -> 160 us (level)
    pallas_call x0 -> x1, Pallas kernels: none -> 7.03 us  [local(): pl.pallas_call(main_kernel, in_specs=[anywhere] * 8, out_specs=[anywhere]...]
    pallas_call x6 -> x5, Pallas kernels: 16 us -> 9.6 us  [call(): pl.pallas_call(body, grid=(grid,), in_specs=[cut(a, d, grid) for a, d in...]
where the time goes in v6:
time: 160 us; the launch traced here: 159 us
  waiting for transfers between devices  103 us (64%)
  starting transfers between devices  31.6 us (20%)
  Pallas kernels  21.7 us (14%)
    all_to_all x2, waiting for transfers between devices, exchange(): lax.all_to_all(flat, 'ctx', split_axis=0, concat_axis=0, tiled=True)  95.6 us
    all_to_all x2, starting transfers between devices, exchange(): lax.all_to_all(flat, 'ctx', split_axis=0, concat_axis=0, tiled=True)  25.3 us
    pallas_call x5, Pallas kernels, call(): pl.pallas_call(body, grid=(grid,), in_specs=[cut(a, d, grid) for a, d in...  9.6 us
    all_to_all x1, waiting for transfers between devices, local(): rows = lax.all_to_all(cuts, 'tp', split_axis=0, concat_axis=0, tiled=True)  7.35 us
    pallas_call x1, Pallas kernels, local(): pl.pallas_call(main_kernel, in_specs=[anywhere] * 8, out_specs=[anywhere]...  7.03 us
    all_to_all x1, starting transfers between devices, local(): rows = lax.all_to_all(cuts, 'tp', split_axis=0, concat_axis=0, tiled=True)  4.3 us
  transfers between devices with their start and end apart: 4, of which 4 were waited for; matrix products, arithmetic and copies ran while one was open for 1% of the time, Pallas kernels for 6%

profile of v6, /device:TPU:8, one launch (start us, length us, event | category | flops | bytes accessed | tf_op | source)
XLA Modules:
  0.0 159.2 jit_solution(6052270139188138572)
XLA Ops:
  0.6 1.8 %shard_map.147 = bf16[4,32,2048]{2,1,0:T(8,128)(2,1)} custom-call(bf16[32,8192]{1,0:T(8,128)(2,1)} %bitcast.30), custom_call_target="tpu_custom_call" | custom-call | tf_op jit(solution)/shard_map/pallas_call | solution.py:283
  2.5 4.3 %all-to-all-start = ((bf16[4,32,2048]{2,1,0:T(8,128)(2,1)}), bf16[4,32,2048]{2,1,0:T(8,128)(2,1)S(1)}, u32[]{:S(2)}, u32[]{:S(2)}) async-start(bf16[4,32,2048]{2,1,0:T(8,128)(2,1)} %shard_map.147), calls=%async_computation | async-start | bytes 1048576 | tf_op jit(solution)/shard_map/all_to_all | solution.py:293
  6.8 2.1 %shard_map.148 = (bf16[64,2,32,128]{3,2,1,0:T(8,128)(2,1)}, bf16[2048,128]{1,0:T(8,128)(2,1)S(1)}) custom-call(bf16[2048,128]{1,0:T(8,128)(2,1)} %bitcast.24, bf16[2048,128]{1,0:T(8,128)(2,1)} %bitcast.26, bf16[2048,128]{1,0:T(8,128)(2,1)} %bitcast.29), custom_call_target="tpu_custom_call" | custom-call | tf_op jit(solution)/shard_map/pallas_call | solution.py:298
  8.9 7.3 %all-to-all-done = bf16[4,32,2048]{2,1,0:T(8,128)(2,1)S(1)} async-done(((bf16[4,32,2048]{2,1,0:T(8,128)(2,1)}), bf16[4,32,2048]{2,1,0:T(8,128)(2,1)S(1)}, u32[]{:S(2)}, u32[]{:S(2)}) %all-to-all-start) | async-done | bytes 524320 | tf_op jit(solution)/shard_map/all_to_all | solution.py:293
  16.3 1.1 shard_map.149.packed
  17.3 0.0 copy-start.2
  17.3 19.0 %all-to-all-start.1 = ((bf16[64,64,128]{2,1,0:T(8,128)(2,1)}), bf16[64,64,128]{2,1,0:T(8,128)(2,1)}, u32[]{:S(2)}, u32[]{:S(2)}) async-start(bf16[64,64,128]{2,1,0:T(8,128)(2,1)} %bitcast.20), calls=%async_computation.1 | async-start | bytes 2097152 | tf_op jit(solution)/shard_map/all_to_all | solution.py:279
  36.4 0.0 copy-done.2
  36.4 0.1 copy.17
  36.5 2.2 %shard_map.150.f_spec = f32[2560,256]{1,0:T(8,128)S(1)} custom-call(bf16[32,64,128]{2,1,0:T(8,128)(2,1)S(1)} %bitcast.23, bf16[160,64]{1,0:T(8,128)(2,1)} %constant.31.clone.fwd.refs_0_, f32[80,256]{1,0:T(8,128)} %constant.33.clone.tc.refs_2_, f32[80,256]{1,0:T(8,128)} %constant.34.clone.ts.refs_3_, bf16[256,256]{1,0:T(8,128)(2,1)} %constant.35.clone.mf.refs_4_), custom_call_target="tpu_custom_call" | custom-call | flops 1048576 | bytes 1048576 | tf_op jit(solution)/shard_map/pallas_call | solution.py:249
  38.8 51.2 %all-to-all-done.1 = bf16[64,64,128]{2,1,0:T(8,128)(2,1)} async-done(((bf16[64,64,128]{2,1,0:T(8,128)(2,1)}), bf16[64,64,128]{2,1,0:T(8,128)(2,1)}, u32[]{:S(2)}, u32[]{:S(2)}) %all-to-all-start.1) | async-done | bytes 1048608 | tf_op jit(solution)/shard_map/all_to_all | solution.py:279
  90.0 7.0 %shard_map.151 = (bf16[64,2,32,128]{3,2,1,0:T(8,128)(2,1)}, bf16[2560,256]{1,0:T(8,128)(2,1)}) custom-call(bf16[64,2,32,128]{3,2,1,0:T(8,128)(2,1)} %bitcast.6.got, f32[2560,256]{1,0:T(8,128)S(1)} %shard_map.150.f_spec, bf16[160,64]{1,0:T(8,128)(2,1)} %constant.31.clone.fwd.refs_0_, bf16[64,160]{1,0:T(8,128)(2,1)} %constant.32.clone.refs_1_, ...), custom_call_target="tpu_custom_call" | custom-call | flops 1048576 | bytes 1048576 | tf_op jit(solution)/shard_map/pallas_call | solution.py:320
  97.0 0.0 copy-start.3
  97.0 0.0 copy-start.1
  97.1 0.0 copy-start.4
  97.1 6.3 %all-to-all-start.2 = ((bf16[64,64,128]{2,1,0:T(8,128)(2,1)}), bf16[64,64,128]{2,1,0:T(8,128)(2,1)}, u32[]{:S(2)}, u32[]{:S(2)}) async-start(bf16[64,64,128]{2,1,0:T(8,128)(2,1)} %bitcast.28), calls=%async_computation.2 | async-start | bytes 2097152 | tf_op jit(solution)/shard_map/all_to_all | solution.py:279
  103.4 0.0 copy-done.3
  103.4 0.6 dynamic-slice_bitcast_fusion
  104.0 0.0 copy-done.1
  104.0 2.3 %shard_map.152 = (f32[32,32,128]{2,1,0:T(8,128)S(1)}, bf16[32,32,128]{2,1,0:T(8,128)(2,1)S(1)}) custom-call(bf16[2560,256]{1,0:T(8,128)(2,1)S(1)} %copy-done.1, bf16[32,160]{1,0:T(8,128)(2,1)} %get-tuple-element.27.own_rows, bf16[32,160]{1,0:T(8,128)(2,1)} %get-tuple-element.26.away_rows, f32[80,256]{1,0:T(8,128)} %constant.33.clone.tc.refs_2_, ...), custom_call_target="tpu_custom_call" | custom-call | flops 1048576 | bytes 1048576 | tf_op jit(solution)/shard_map/pallas_call | solution.py:249
  106.3 1.9 %collective-permute-start = (bf16[32,32,128]{2,1,0:T(8,128)(2,1)S(1)}, bf16[32,32,128]{2,1,0:T(8,128)(2,1)S(1)}, u32[]{:S(2)}, u32[]{:S(2)}) collective-permute-start(bf16[32,32,128]{2,1,0:T(8,128)(2,1)S(1)} %get-tuple-element.20), channel_id=1, source_target_pairs={{0,256},{256,0},{1,257},{257,1},{2,258},{258,2},{3,259},{259,3},{4... | collective-permute-start | bytes 786440 | tf_op jit(solution)/shard_map/ppermute | solution.py:351
  108.2 0.5 broadcast.4
  108.7 0.0 copy-done.4
  108.7 0.7 reduce.3
  109.4 0.1 reshape_squeeze.7.skip
  109.5 0.2 collective-permute-done.other
  109.7 0.9 shard_map.153
  110.6 0.0 copy-start
  110.6 1.6 %shard_map.154.near = bf16[3,2048,128]{2,1,0:T(8,128)(2,1)S(1)} custom-call(bf16[128,2048]{1,0:T(8,128)(2,1)S(1)} %bitcast.22, bf16[2048,128]{1,0:T(8,128)(2,1)} %bitcast.25, bf16[2048,128]{1,0:T(8,128)(2,1)} %bitcast.27), custom_call_target="tpu_custom_call" | custom-call | flops 1048576 | bytes 1048576 | tf_op jit(solution)/shard_map/pallas_call | solution.py:249
  112.2 44.4 %all-to-all-done.2 = bf16[64,64,128]{2,1,0:T(8,128)(2,1)} async-done(((bf16[64,64,128]{2,1,0:T(8,128)(2,1)}), bf16[64,64,128]{2,1,0:T(8,128)(2,1)}, u32[]{:S(2)}, u32[]{:S(2)}) %all-to-all-start.2) | async-done | bytes 1048608 | tf_op jit(solution)/shard_map/all_to_all | solution.py:279
  156.6 0.0 copy-done
  156.6 2.6 %shard_map.155 = (bf16[2048,128]{1,0:T(8,128)(2,1)}, bf16[2048,128]{1,0:T(8,128)(2,1)}, bf16[2048,128]{1,0:T(8,128)(2,1)}) custom-call(bf16[64,2,32,128]{3,2,1,0:T(8,128)(2,1)} %bitcast.8.both, bf16[64,2,32,128]{3,2,1,0:T(8,128)(2,1)S(1)} %copy-done, bf16[3,2048,128]{2,1,0:T(8,128)(2,1)S(1)} %shard_map.154.near, f32[64,32]{1,0:T(8,128)S(1)} %reshape_squeeze.7.skip), custom_call_target="tpu_custom_call" | custom-call | flops 1048576 | bytes 1048576 | tf_op jit(solution)/shard_map/pallas_call | solution.py:249
Async XLA Ops:
  2.5 13.8 %all-to-all-start = ((bf16[4,32,2048]{2,1,0:T(8,128)(2,1)}), bf16[4,32,2048]{2,1,0:T(8,128)(2,1)S(1)}, u32[]{:S(2)}, u32[]{:S(2)}) async-start(bf16[4,32,2048]{2,1,0:T(8,128)(2,1)} %shard_map.147), calls=%async_computation | async-start | bytes 1048576 | tf_op jit(solution)/shard_map/all_to_all | solution.py:293
  17.3 19.1 %copy-start.2 = (bf16[1,32,8192]{2,1,0:T(8,128)(2,1)S(1)}, bf16[1,32,8192]{2,1,0:T(8,128)(2,1)}, u32[]{:S(2)}) copy-start(bf16[1,32,8192]{2,1,0:T(8,128)(2,1)} %param.16) | copy-start | bytes 1572868
  17.3 72.7 %all-to-all-start.1 = ((bf16[64,64,128]{2,1,0:T(8,128)(2,1)}), bf16[64,64,128]{2,1,0:T(8,128)(2,1)}, u32[]{:S(2)}, u32[]{:S(2)}) async-start(bf16[64,64,128]{2,1,0:T(8,128)(2,1)} %bitcast.20), calls=%async_computation.1 | async-start | bytes 2097152 | tf_op jit(solution)/shard_map/all_to_all | solution.py:279
  97.0 6.3 %copy-start.3 = (bf16[2,32,160]{2,1,0:T(8,128)(2,1)S(1)}, bf16[2,32,160]{2,1,0:T(8,128)(2,1)}, u32[]{:S(2)}) copy-start(bf16[2,32,160]{2,1,0:T(8,128)(2,1)} %constant.43) | copy-start | bytes 61444
  97.0 7.0 %copy-start.1 = (bf16[2560,256]{1,0:T(8,128)(2,1)S(1)}, bf16[2560,256]{1,0:T(8,128)(2,1)}, u32[]{:S(2)}) copy-start(bf16[2560,256]{1,0:T(8,128)(2,1)} %get-tuple-element.18.lag_spec) | copy-start | bytes 3932164
  97.1 11.7 %copy-start.4 = (f32[1,2048]{1,0:T(1,128)S(1)}, f32[1,2048]{1,0:T(1,128)}, u32[]{:S(2)}) copy-start(f32[1,2048]{1,0:T(1,128)} %param.17) | copy-start | bytes 24580
  97.1 59.5 %all-to-all-start.2 = ((bf16[64,64,128]{2,1,0:T(8,128)(2,1)}), bf16[64,64,128]{2,1,0:T(8,128)(2,1)}, u32[]{:S(2)}, u32[]{:S(2)}) async-start(bf16[64,64,128]{2,1,0:T(8,128)(2,1)} %bitcast.28), calls=%async_computation.2 | async-start | bytes 2097152 | tf_op jit(solution)/shard_map/all_to_all | solution.py:279
  106.3 3.4 %collective-permute-start = (bf16[32,32,128]{2,1,0:T(8,128)(2,1)S(1)}, bf16[32,32,128]{2,1,0:T(8,128)(2,1)S(1)}, u32[]{:S(2)}, u32[]{:S(2)}) collective-permute-start(bf16[32,32,128]{2,1,0:T(8,128)(2,1)S(1)} %get-tuple-element.20), channel_id=1, source_target_pairs={{0,256},{256,0},{1,257},{257,1},{2,258},{258,2},{3,259},{259,3},{4... | collective-permute-start | bytes 786440 | tf_op jit(solution)/shard_map/ppermute | solution.py:351
  110.6 46.0 %copy-start = (bf16[64,2,32,128]{3,2,1,0:T(8,128)(2,1)S(1)}, bf16[64,2,32,128]{3,2,1,0:T(8,128)(2,1)}, u32[]{:S(2)}) copy-start(bf16[64,2,32,128]{3,2,1,0:T(8,128)(2,1)} %shard_map.149.packed) | copy-start | bytes 3145732
